TPU v7x, 512 devices: a whole 4x8x8 slice. The times are simulated.
512 devices in a mesh: lon: 64 (over x, y_hi, z), tp: 8 (over y_lo, core).
Axes of the slice: x: 4, y: 8 (y_hi: 2, y_lo: 4; y = y_hi * 4 + y_lo), z: 8, core: 2. Of those that a mesh axis runs over, the one named last changes fastest.
Arguments:
- qkv: bfloat16 [3, 65536, 2048], P(None, 'lon', 'tp'), may hold values from -5 to 5
- windows: int32 [512, 4], P('lon'), may hold values from 1 to 47, as said below
- out_weight: bfloat16 [2048, 2048], P('tp'), may hold values from -0.125 to 0.125
- cotangent: bfloat16 [65536, 2048], P(('lon', 'tp')), may hold values from -6 to 6
Outputs:
- mixed_rows: bfloat16 [65536, 2048], P(('lon', 'tp'))
- grad_qkv: bfloat16 [3, 65536, 2048], P(None, 'lon', 'tp')
Inputs may be any that keep to these rules, and one draw needn't show every extreme that they name: `windows`: for each sector, its 8 rows list 2 x 2 blocks of tiles: tile rows r and (r + 1) mod 16 and tile columns c and c + 1 with c odd, column 2 meaning column 0 of the next sector east (entry 32 + r). r has one parity within a sector. Together the rows cover each such tile exactly once, the sector's column 0 never; rows and the four entries of a row come in any order.
All inputs are finite; a program needn't handle non-finite values.
Results may differ from a plain program's by a relative error of at most 0.017.
Values may be sent and summed in bfloat16 or wider, within the bound.
A program may use at most 64 MiB of HBM per device.

v0:
```python
import jax
import jax.numpy as jnp
from jax import lax
from jax.sharding import PartitionSpec as P

HEAD_DIM = 128
TILE = 32
LON_TILES = 2
LAT_TILES = 16


def shifted(value, axis, steps):
    count = lax.axis_size(axis)
    pairs = [(source, (source + steps) % count) for source in range(count)]
    return lax.ppermute(value, axis, pairs)


def window_pass(queries, key_rows, value_rows, grad_out):
    score_scale = HEAD_DIM ** (-0.5)
    scores = (
        jnp.einsum("wqhd,wkhd->whqk", queries, key_rows, preferred_element_type=jnp.float32)
        * score_scale
    )
    row_max = jnp.max(scores, axis=-1, keepdims=True)
    raised = jnp.exp(scores - row_max)
    weights = raised / jnp.sum(raised, axis=-1, keepdims=True)
    weights_low = weights.astype(jnp.bfloat16)
    attended = jnp.einsum(
        "whqk,wkhd->wqhd", weights_low, value_rows, preferred_element_type=jnp.float32
    ).astype(jnp.bfloat16)
    grad_values = jnp.einsum(
        "whqk,wqhd->wkhd", weights_low, grad_out, preferred_element_type=jnp.float32
    ).astype(jnp.bfloat16)
    grad_weights = jnp.einsum(
        "wqhd,wkhd->whqk", grad_out, value_rows, preferred_element_type=jnp.float32
    )
    row_dot = jnp.sum(weights * grad_weights, axis=-1, keepdims=True)
    grad_scores = (weights * (grad_weights - row_dot) * score_scale).astype(jnp.bfloat16)
    grad_queries = jnp.einsum(
        "whqk,wkhd->wqhd", grad_scores, key_rows, preferred_element_type=jnp.float32
    ).astype(jnp.bfloat16)
    grad_keys = jnp.einsum(
        "whqk,wqhd->wkhd", grad_scores, queries, preferred_element_type=jnp.float32
    ).astype(jnp.bfloat16)
    return (attended, grad_queries, grad_keys, grad_values)


def run_windows(source, tile_list, window_count, head_count, slot_count):
    feature_width = source.shape[-1]
    gathered = jnp.take(source, tile_list, axis=1).reshape(
        4, window_count, 4 * TILE, head_count, HEAD_DIM
    )
    results = window_pass(gathered[0], gathered[1], gathered[2], gathered[3])
    stacked = jnp.stack(results).reshape(4, window_count * 4, TILE, feature_width)
    return (
        jnp.zeros((4, slot_count, TILE, feature_width), jnp.bfloat16).at[:, tile_list].set(stacked)
    )


def per_device(qkv, windows, out_weight, cotangent):
    feature_width = qkv.shape[2]
    token_count = qkv.shape[1]
    head_count = feature_width // HEAD_DIM
    window_count = windows.shape[0]
    tile_count = LAT_TILES * LON_TILES
    grad_out = lax.dot_general(
        lax.all_gather(cotangent, "tp", axis=0, tiled=True),
        out_weight,
        (((1,), (1,)), ((), ())),
        preferred_element_type=jnp.float32,
    ).astype(jnp.bfloat16)
    layout = jnp.concatenate([qkv, grad_out[None]], axis=0)
    tiled_all = layout.reshape(4, LAT_TILES, LON_TILES, TILE, feature_width)
    borrowed = shifted(tiled_all[:, :, 0], "lon", -1)
    extended = jnp.concatenate(
        [layout.reshape(4, tile_count, TILE, feature_width), borrowed], axis=1
    )
    placed = run_windows(
        extended, windows.reshape(-1), window_count, head_count, tile_count + LAT_TILES
    )
    returned = shifted(placed[:, tile_count:], "lon", 1)
    home_tiles = placed[:, :tile_count].reshape(4, LAT_TILES, LON_TILES, TILE, feature_width)
    home_tiles = home_tiles.at[:, :, 0].set(returned).reshape(4, token_count, feature_width)
    attended = home_tiles[0]
    mixed_rows = lax.psum_scatter(
        jnp.dot(attended, out_weight, preferred_element_type=jnp.float32).astype(jnp.bfloat16),
        "tp",
        scatter_dimension=0,
        tiled=True,
    )
    return (mixed_rows, home_tiles[1:])


def solution(mesh):
    in_specs = (P(None, "lon", "tp"), P("lon", None), P("tp", None), P(("lon", "tp"), None))
    out_specs = (P(("lon", "tp"), None), P(None, "lon", "tp"))
    return jax.shard_map(
        per_device, mesh=mesh, in_specs=in_specs, out_specs=out_specs, check_vma=False
    )
```

profile of v0, /device:TPU:1, one launch (start us, length us, event | category | flops | bytes accessed | tf_op | source)
XLA Modules:
  0.0 285.8 jit_solution(3012407024483610018)
XLA Ops:
  7.2 0.7 all-gather.2.cloned.1.call-update
  8.0 62.8 %all-gather.2.cloned.1.call-done = bf16[1024,2048]{1,0:T(8,128)(2,1)} async-done(((bf16[128,2048]{1,0:T(8,128)(2,1)}), bf16[1024,2048]{1,0:T(8,128)(2,1)}) %all-gather.2.cloned.1.call-update) | async-done | bytes 4194320 | tf_op jit(solution)/shard_map/all_gather | solution.py:67
  70.8 3.5 %convolution_convert_fusion.5 = bf16[1024,256]{1,0:T(8,128)(2,1)S(1)} fusion(bf16[1024,2048]{1,0:T(8,128)(2,1)} %all-gather.2.cloned.1.call-done, bf16[256,2048]{1,0:T(8,128)(2,1)S(1)} %copy-done), kind=kOutput, calls=%fused_computation.19 | convolution fusion | flops 1074003968 | bytes 5767168 | tf_op jit(solution)/shard_map/dot_general | solution.py:66
  74.3 1.1 fusion.12
  75.4 12.2 %collective-permute-start = (bf16[4,16,32,256]{3,2,1,0:T(8,128)(2,1)}, bf16[4,16,32,256]{3,2,1,0:T(8,128)(2,1)}, u32[]{:S(2)}, u32[]{:S(2)}) collective-permute-start(bf16[4,16,32,256]{3,2,1,0:T(8,128)(2,1)} %fusion.12), channel_id=1, source_target_pairs={{0,504},{8,0},{16,8},{24,16},{32,24},{40,32},{48,40},{56,48},{64,5... | collective-permute-start | bytes 3145736 | tf_op jit(solution)/shard_map/ppermute | solution.py:15
  87.9 44.8 %collective-permute-done = bf16[4,16,32,256]{3,2,1,0:T(8,128)(2,1)} collective-permute-done((bf16[4,16,32,256]{3,2,1,0:T(8,128)(2,1)}, bf16[4,16,32,256]{3,2,1,0:T(8,128)(2,1)}, u32[]{:S(2)}, u32[]{:S(2)}) %collective-permute-start) | collective-permute-done | bytes 1048608 | tf_op jit(solution)/shard_map/ppermute | solution.py:15
  132.7 3.2 %pad_maximum_fusion = bf16[4,48,32,256]{3,2,1,0:T(8,128)(2,1)} fusion(bf16[4,16,32,256]{3,2,1,0:T(8,128)(2,1)} %collective-permute-done, bf16[1,32,32,256]{3,2,1,0:T(8,128)(2,1)S(1)} %bitcast.61, bf16[3,32,32,256]{3,2,1,0:T(8,128)(2,1)S(1)} %bitcast.58), kind=kLoop, calls=%fused_computation.5 | loop fusion | flops 3145728 | bytes 6291456 | tf_op jit(solution)/shard_map/concatenate | solution.py:75
  135.9 2.6 gather_fusion
  138.8 1.2 fusion.31
  140.2 0.4 copy.73
  140.6 1.2 squeeze.21
  142.3 1.2 squeeze.20
  143.4 1.1 copy.70
  144.5 1.3 fusion.20
  145.8 1.5 fusion.32
  147.3 3.5 %fusion.9 = bf16[8,128,2,128]{1,3,2,0:T(8,128)(2,1)} fusion(bf16[8,128,2,128]{1,3,2,0:T(8,128)(2,1)S(1)} %copy.67, f32[8,2,128,128]{2,3,1,0:T(8,128)} %fusion.20, f32[8,2,128,128]{2,3,1,0:T(8,128)} %get-tuple-element.19, f32[8,2,128]{2,1,0:T(2,128)S(1)} %get-tuple-element.18), kind=kOutput, calls=%fused_computation.21 | convolution fusion | flops 69208192 | bytes 3153920 | tf_op jit(solution)/shard_map/whqk,wkhd->wqhd/dot_general | solution.py:39
  150.8 2.7 fusion.10
  153.5 2.6 fusion.11
  156.1 1.1 fusion.8
  159.0 1.3 copy.64
  160.7 1.3 copy.75
  162.0 1.1 stack.18
  163.1 1.3 maximum_bitcast_fusion
  164.6 2.1 broadcast_in_dim.18
  166.7 5.5 %scatter_fusion = bf16[4,48,32,256]{3,2,1,0:T(8,128)(2,1)} fusion(bf16[4,48,32,256]{3,2,1,0:T(8,128)(2,1)} %broadcast_in_dim.18, s32[32]{0:T(128)S(1)} %fusion.24, bf16[32,4,32,256]{3,2,1,0:T(8,128)(2,1)S(1)} %copy.76), kind=kCustom, calls=%fused_computation.1 | custom fusion | bytes 6291584 | tf_op jit(solution)/shard_map/scatter | solution.py:56
  172.1 1.3 slice.82
  173.4 1.9 collective-permute-start.1
  175.4 1.8 slice.81
  177.1 53.4 %collective-permute-done.1 = bf16[4,16,32,256]{3,2,1,0:T(8,128)(2,1)S(1)} collective-permute-done((bf16[4,16,32,256]{3,2,1,0:T(8,128)(2,1)S(1)}, bf16[4,16,32,256]{3,2,1,0:T(8,128)(2,1)S(1)}, u32[]{:S(2)}, u32[]{:S(2)}) %collective-permute-start.1) | collective-permute-done | bytes 1048608 | tf_op jit(solution)/shard_map/ppermute | solution.py:15
  230.6 3.2 %convolution_convert_fusion = bf16[1024,2048]{1,0:T(8,128)(2,1)} fusion(bf16[1024,256]{1,0:T(8,128)(2,1)S(1)} %bitcast.59, bf16[256,2048]{1,0:T(8,128)(2,1)S(1)} %copy-done), kind=kOutput, calls=%fused_computation.4 | convolution fusion | flops 1075838976 | bytes 5767168 | tf_op jit(solution)/shard_map/dot_general | solution.py:86
  233.8 1.3 slice.84
  235.1 43.8 %reduce-scatter.2.cloned.1.call-done = bf16[128,2048]{1,0:T(8,128)(2,1)} async-done(((bf16[1024,2048]{1,0:T(8,128)(2,1)}), bf16[128,2048]{1,0:T(8,128)(2,1)}) %reduce-scatter.2.cloned.1.call-update) | async-done | bytes 524304 | tf_op jit(solution)/shard_map/reduce_scatter | solution.py:85
  (33 shorter events, 3.7 us)
Async XLA Ops:
  7.2 63.7 %copy-start = (bf16[256,2048]{1,0:T(8,128)(2,1)S(1)}, bf16[256,2048]{1,0:T(8,128)(2,1)}, u32[]{:S(2)}) copy-start(bf16[256,2048]{1,0:T(8,128)(2,1)} %param.8) | copy-start | bytes 3145732
  7.2 63.6 %all-gather.2.cloned.1.call-start = ((), (), s32[]{:S(2)}) async-start(), calls=%async_computation.1 | async-start | bytes 4718592 | tf_op jit(solution)/shard_map/all_gather | solution.py:67
  7.9 66.4 %copy-start.1 = (bf16[3,1024,256]{2,1,0:T(8,128)(2,1)S(1)}, bf16[3,1024,256]{2,1,0:T(8,128)(2,1)}, u32[]{:S(2)}) copy-start(bf16[3,1024,256]{2,1,0:T(8,128)(2,1)} %param.6) | copy-start | bytes 4718596
  7.9 271.0 %reduce-scatter.2.cloned.1.call-start = ((), (), s32[]{:S(2)}) async-start(), calls=%async_computation.2 | async-start | bytes 4718592 | tf_op jit(solution)/shard_map/reduce_scatter | solution.py:85
  74.3 13.3 %copy-start.5 = (s32[8,4]{0,1:T(4,128)S(1)}, s32[8,4]{0,1:T(4,128)}, u32[]{:S(2)}) copy-start(s32[8,4]{0,1:T(4,128)} %param.7) | copy-start | bytes 388
  75.4 57.3 %collective-permute-start = (bf16[4,16,32,256]{3,2,1,0:T(8,128)(2,1)}, bf16[4,16,32,256]{3,2,1,0:T(8,128)(2,1)}, u32[]{:S(2)}, u32[]{:S(2)}) collective-permute-start(bf16[4,16,32,256]{3,2,1,0:T(8,128)(2,1)} %fusion.12), channel_id=1, source_target_pairs={{0,504},{8,0},{16,8},{24,16},{32,24},{40,32},{48,40},{56,48},{64,5... | collective-permute-start | bytes 3145736 | tf_op jit(solution)/shard_map/ppermute | solution.py:15
  144.5 1.3 copy-start.2
  153.5 2.6 copy-start.3
  157.2 1.0 copy-start.4
  173.4 57.1 %collective-permute-start.1 = (bf16[4,16,32,256]{3,2,1,0:T(8,128)(2,1)S(1)}, bf16[4,16,32,256]{3,2,1,0:T(8,128)(2,1)S(1)}, u32[]{:S(2)}, u32[]{:S(2)}) collective-permute-start(bf16[4,16,32,256]{3,2,1,0:T(8,128)(2,1)S(1)} %slice.82), channel_id=1, source_target_pairs={{0,8},{8,16},{16,24},{24,32},{32,40},{40,48},{48,56},{56,64},{64,7... | collective-permute-start | bytes 3145736 | tf_op jit(solution)/shard_map/ppermute | solution.py:15
Sparse Core Ops, SparseCore 0:
  10.1 60.6 all-gather.1
  234.0 44.9 reduce-scatter.1
where the time goes:
time: 288 us; the launch traced here: 286 us
  waiting for transfers between devices  206 us (72%)
  local copies, waits for them, and re-layouts  26.5 us (9%)
  matrix products  19.4 us (7%)
  between operations  14.3 us (5%)
  starting transfers between devices  14.2 us (5%)
  other arithmetic  5.88 us (2%)
    ppermute x2, waiting for transfers between devices, shifted(): return lax.ppermute(value, axis, pairs)  98.1 us
    all_gather x1, waiting for transfers between devices, per_device(): lax.all_gather(cotangent, 'tp', axis=0, tiled=True)  62.8 us
    reduce_scatter x1, waiting for transfers between devices, per_device(): lax.psum_scatter(jnp.dot(attended, out_weight, preferred_element_type=jnp...  43.8 us
    ppermute x2, starting transfers between devices, shifted(): return lax.ppermute(value, axis, pairs)  14.2 us
  transfers between devices with their start and end apart: 4, of which 4 were waited for; matrix products, arithmetic and copies ran while one was open for 1% of the time, Pallas kernels for 0%

commit v1 on v0

v1 whole, which is shorter than its diff:
```python
import functools

import jax
import jax.numpy as jnp
from jax import lax
from jax.experimental import pallas as pl
from jax.experimental.pallas import tpu as pltpu
from jax.sharding import PartitionSpec as P

HEAD_DIM = 128
TILE = 32
ROWS = 16
WINDOWS = 8
WIDTH = 256
D = 2048
OWN = 128
HALF = 64
SCALE = HEAD_DIM ** (-0.5)
MESH = pl.DeviceIdType.MESH
BF16 = jnp.bfloat16
F32 = jnp.float32

NT = (((1,), (1,)), ((), ()))
NN = (((1,), (0,)), ((), ()))
TN = (((0,), (0,)), ((), ()))


def dot(a, b, dims):
    return lax.dot_general(a, b, dims, preferred_element_type=F32)


def kernel(
    n_lon,
    mask_ref, qkv_ref, weight_ref, cot_ref,
    mixed_ref, grad_ref,
    west_mask, kv_east, kv_west, gathered, grad_out, q_win, k_win, v_win, do_win,
    weights, out_win, attended, dq_win, dk_own, dv_own, dk_far, dv_far,
    dkv_send, dkv_east, dkv_west, part_out, part_in, part, from_near, from_far,
    lon_send, lon_recv, tp_send, tp_recv, sib_send, sib_recv,
    part_send, part_recv, sum_send, sum_recv,
):
    lon, tp = lax.axis_index("lon"), lax.axis_index("tp")
    chip, core = tp // 2, tp % 2
    east = {"lon": lax.rem(lon + 1, n_lon)}
    west = {"lon": lax.rem(lon + n_lon - 1, n_lon)}
    flip = chip // 2
    pos = chip + flip * (3 - 2 * chip)
    edge, inner = pos == 0, pos == 1

    def chip_at(place):
        return place + flip * (3 - 2 * place)

    def device_at(place, which):
        return 2 * chip_at(place) + which

    near = {"tp": device_at(0, core)}
    one = {"tp": device_at(1, core)}
    far = {"tp": device_at(2, core)}
    sibling = {"tp": 2 * chip + 1 - core}

    barrier = pltpu.get_barrier_semaphore()
    for target in (east, west, sibling):
        pl.semaphore_signal(barrier, inc=1, device_id=target, device_id_type=MESH)

    @pl.when(edge)
    def _():
        pl.semaphore_signal(barrier, inc=1, device_id=one, device_id_type=MESH)
        pl.semaphore_wait(barrier, 4)

    @pl.when(inner)
    def _():
        pl.semaphore_signal(barrier, inc=1, device_id=near, device_id_type=MESH)
        pl.semaphore_signal(barrier, inc=1, device_id=far, device_id_type=MESH)
        pl.semaphore_wait(barrier, 5)

    def remote(src, dst, send_sem, recv_sem, target):
        return pltpu.make_async_remote_copy(
            src_ref=src, dst_ref=dst, send_sem=send_sem, recv_sem=recv_sem,
            device_id=target, device_id_type=MESH,
        )

    pending = []

    def start(copy, condition=None):
        if condition is None:
            copy.start()
        else:
            pl.when(condition)(copy.start)
        pending.append((copy, condition))

    mask_copy = remote(mask_ref, west_mask, lon_send.at[0], lon_recv.at[0], east)
    start(mask_copy)
    to_west = remote(qkv_ref.at[pl.ds(1, 2), :, 0], kv_east, lon_send.at[1], lon_recv.at[1], west)
    to_east = remote(qkv_ref.at[pl.ds(1, 2), :, 1], kv_west, lon_send.at[2], lon_recv.at[2], east)
    start(to_west)
    start(to_east)

    def block(place, which, half):
        return gathered.at[device_at(place, which), half]

    def own_half(half):
        return cot_ref.at[pl.ds(half * HALF, HALF)]

    def slot(place, half):
        return 2 * place + half

    for half in range(2):
        start(remote(own_half(half), gathered.at[tp, half], tp_send.at[half],
                     tp_recv.at[slot(0, half)], one), edge)
        start(remote(own_half(half), gathered.at[tp, half], tp_send.at[half],
                     tp_recv.at[slot(1, half)], near), inner)
        start(remote(own_half(half), gathered.at[tp, half], tp_send.at[2 + half],
                     tp_recv.at[slot(2, half)], far), inner)
        start(remote(own_half(half), gathered.at[tp, half], sib_send.at[half],
                     sib_recv.at[half], sibling))

    def wait_tp(place, half):
        remote(block(place, core, half), block(place, core, half), tp_send.at[0],
               tp_recv.at[slot(place, half)], sibling).wait_recv()

    def hand_over(place, half, order):
        src = block(place, core, half)
        return remote(src, src, sib_send.at[2 * order + half], sib_recv.at[2 * order + half], sibling)

    def gather_step(order, half):
        if order == 1:
            @pl.when(edge)
            def _():
                wait_tp(1, half)
            start(hand_over(1, half, 1), edge)

            @pl.when(inner)
            def _():
                wait_tp(2, half)
            start(remote(block(2, core, half), block(2, core, half), tp_send.at[4 + half],
                         tp_recv.at[slot(2, half)], near), inner)
            start(hand_over(2, half, 1), inner)

            @pl.when(inner)
            def _():
                wait_tp(0, half)
            start(remote(block(0, core, half), block(0, core, half), tp_send.at[6 + half],
                         tp_recv.at[slot(3, half)], far), inner)
            start(hand_over(0, half, 2), inner)
        else:
            place = order
            if order == 2:
                @pl.when(edge)
                def _():
                    wait_tp(2, half)
                start(hand_over(2, half, 2), edge)

                @pl.when(inner)
                def _():
                    wait_tp(3, half)
                start(remote(block(3, core, half), block(3, core, half), tp_send.at[8 + half],
                             tp_recv.at[slot(3, half)], near), inner)
                start(hand_over(3, half, 3), inner)
            else:
                @pl.when(edge)
                def _():
                    wait_tp(3, half)
                start(hand_over(3, half, 3), edge)

    def place_of(order):
        return (pos, 1 + pos, 2 - 2 * pos, 3)[order]

    def wait_hand_over(order):
        for half in range(2):
            dst = gathered.at[device_at(place_of(order), 1 - core), half]
            remote(dst, dst, sib_send.at[0], sib_recv.at[2 * order + half], sibling).wait_recv()

    def project_back(src_rows, device):
        def body(index, carry):
            rows = src_rows(index)
            value = dot(rows, weight_ref[...], NT).astype(BF16)
            grad_out[2 * device + index] = value.reshape(2, TILE, WIDTH)
            return carry
        lax.fori_loop(0, 2, body, 0)

    def project_order(order):
        if order == 0:
            project_back(lambda i: cot_ref[pl.ds(i * HALF, HALF), :], tp)
        else:
            device = device_at(place_of(order), core)
            project_back(lambda i: gathered[device, i], device)
        wait_hand_over(order)
        other = device_at(place_of(order), 1 - core)
        project_back(lambda i: gathered[other, i], other)

    def mask_of(col):
        return (west_mask, mask_ref)[col]

    def into_windows(col, pairs):
        def body(row, carry):
            later = lax.rem(row + 1, ROWS)
            take = mask_of(col)[...] > 0
            for read, write in pairs:
                write(row, jnp.where(take, read(later), read(row)))
            return carry
        lax.fori_loop(0, ROWS, body, 0)

    def from_windows(col, pairs, dtype):
        def body(row, carry):
            before = lax.rem(row + ROWS - 1, ROWS)
            take = mask_of(col)[...].astype(dtype) > 0
            for read, write in pairs:
                write(row, jnp.where(take, read(before), read(row)))
            return carry
        lax.fori_loop(0, ROWS, body, 0)

    def put_query(ref, col):
        def write(row, value):
            ref[col, pl.ds(pl.multiple_of(row * TILE, TILE), TILE), :] = value
        return write

    def put_key(ref, col, remote_half):
        def write(row, value):
            window, part_of = row // 2, row % 2
            place = window * 128 + remote_half * 64 + part_of * TILE
            ref[col, pl.ds(pl.multiple_of(place, TILE), TILE), :] = value
        return write

    def get_window(ref, col):
        return lambda row: ref[col, pl.ds(pl.multiple_of(row * TILE, TILE), TILE), :]

    def own_into_windows(col):
        into_windows(col, [
            (lambda row: qkv_ref[0, row, col], put_query(q_win, col)),
            (lambda row: qkv_ref[1, row, col], put_key(k_win, col, 0)),
            (lambda row: qkv_ref[2, row, col], put_key(v_win, col, 0)),
        ])

    def far_into_windows(col):
        kv = (kv_west, kv_east)[col]
        into_windows(col, [
            (lambda row: kv[0, row], put_key(k_win, col, 1)),
            (lambda row: kv[1, row], put_key(v_win, col, 1)),
        ])

    def forward():
        def body(window, carry):
            qs = pl.ds(pl.multiple_of(window * 64, 64), 64)
            ks = pl.ds(pl.multiple_of(window * 128, 128), 128)
            for col in range(2):
                for head in range(2):
                    lanes = slice(head * HEAD_DIM, (head + 1) * HEAD_DIM)
                    scores = dot(q_win[col, qs, lanes], k_win[col, ks, lanes], NT) * SCALE
                    raised = jnp.exp(scores - jnp.max(scores, axis=-1, keepdims=True))
                    probs = raised / jnp.sum(raised, axis=-1, keepdims=True)
                    weights[col, head, qs, :] = probs
                    out_win[col, qs, lanes] = dot(
                        probs.astype(BF16), v_win[col, ks, lanes], NN
                    ).astype(BF16)
            return carry
        lax.fori_loop(0, WINDOWS, body, 0)

    def backward():
        def body(window, carry):
            qs = pl.ds(pl.multiple_of(window * 64, 64), 64)
            ks = pl.ds(pl.multiple_of(window * 128, 128), 128)
            for col in range(2):
                for head in range(2):
                    lanes = slice(head * HEAD_DIM, (head + 1) * HEAD_DIM)
                    probs = weights[col, head, qs, :]
                    d_out = do_win[col, qs, lanes]
                    grad_w = dot(d_out, v_win[col, ks, lanes], NT)
                    row_dot = jnp.sum(probs * grad_w, axis=-1, keepdims=True)
                    grad_s = (probs * (grad_w - row_dot) * SCALE).astype(BF16)
                    dq_win[col, qs, lanes] = dot(grad_s, k_win[col, ks, lanes], NN).astype(BF16)
                    dk = dot(grad_s, q_win[col, qs, lanes], TN)
                    dv = dot(probs.astype(BF16), d_out, TN)
                    dk_own[col, qs, lanes] = dk[:64]
                    dv_own[col, qs, lanes] = dv[:64]
                    dk_far[col, qs, lanes] = dk[64:].astype(BF16)
                    dv_far[col, qs, lanes] = dv[64:].astype(BF16)
            return carry
        lax.fori_loop(0, WINDOWS, body, 0)

    def project(rows_of, dst):
        rows = attended[pl.ds(2 * rows_of, 2)].reshape(OWN, WIDTH)

        def body(index, carry):
            cols = pl.ds(pl.multiple_of(index * 512, 512), 512)
            value = dot(rows, weight_ref[:, cols], NN).astype(BF16)
            dst[0, :, cols] = value[:HALF]
            dst[1, :, cols] = value[HALF:]
            return carry
        lax.fori_loop(0, D // 512, body, 0)

    def add(total, other):
        def body(index, carry):
            cols = pl.ds(pl.multiple_of(index * 512, 512), 512)
            total[:, cols] = (total[:, cols].astype(F32) + other[:, cols].astype(F32)).astype(BF16)
            return carry
        lax.fori_loop(0, D // 512, body, 0)

    def part_copy(place):
        return remote(part_out.at[place], part_in.at[place], part_send.at[place],
                      part_recv.at[place], sibling)

    def partials(place):
        project(device_at(place, 1 - core), part_out.at[place])
        start(part_copy(place))
        project(device_at(place, core), part.at[place])

    def join_cores(place):
        part_copy(place).wait_recv()
        for half in range(2):
            add(part.at[place, half], part_in.at[place, half])

    def near_sem(place, half):
        return sum_recv.at[2 * (place - 1) + half]

    def far_sem(place, half):
        return sum_recv.at[6 + 2 * place + half]

    def send_edge(place):
        for half in range(2):
            start(remote(part.at[place, half], from_near.at[place - 1, half],
                         sum_send.at[2 * (place - 1) + half], near_sem(place, half), one), edge)

    def wait_near(place, half):
        ref = from_near.at[place - 1, half]
        remote(ref, ref, sum_send.at[0], near_sem(place, half), sibling).wait_recv()

    def wait_far(place, half):
        ref = from_far.at[place, half]
        remote(ref, ref, sum_send.at[0], far_sem(place, half), sibling).wait_recv()

    def pass_far(place, half):
        @pl.when(inner)
        def _():
            wait_near(place, half)
            add(part.at[place, half], from_near.at[place - 1, half])
        start(remote(part.at[place, half], from_far.at[3 - place, half],
                     sum_send.at[2 * (place - 2) + half], far_sem(3 - place, half), far), inner)

    def pass_near(half):
        @pl.when(inner)
        def _():
            wait_far(0, half)
            add(part.at[0, half], from_far.at[0, half])
        start(remote(part.at[0, half], from_far.at[0, half],
                     sum_send.at[4 + half], far_sem(0, half), near), inner)

    project_order(0)
    own_into_windows(1)
    mask_copy.wait_recv()
    own_into_windows(0)
    gather_step(1, 0)
    gather_step(1, 1)
    project_order(1)
    to_west.wait_recv()
    far_into_windows(1)
    to_east.wait_recv()
    far_into_windows(0)
    forward()
    gather_step(2, 0)
    for col in range(2):
        def put_attended(row, value, col=col):
            attended[row, col] = value
        from_windows(col, [(get_window(out_win, col), put_attended)], BF16)
    partials(3)
    partials(2)
    join_cores(3)
    send_edge(3)
    gather_step(2, 1)
    partials(0)
    partials(1)
    join_cores(2)
    send_edge(2)
    join_cores(1)
    send_edge(1)
    join_cores(0)
    project_order(2)
    gather_step(3, 0)
    pass_far(3, 0)
    gather_step(3, 1)
    pass_far(3, 1)
    project_order(3)
    for col in range(2):
        into_windows(col, [(lambda row, col=col: grad_out[row, col], put_query(do_win, col))])
    pass_near(0)
    pass_far(2, 0)
    pass_near(1)
    pass_far(2, 1)
    backward()
    returns = []
    for col in range(2):
        def put_far(which, col=col):
            def write(row, value):
                dkv_send[col, which, row] = value
            return write
        from_windows(col, [(get_window(dk_far, col), put_far(0)), (get_window(dv_far, col), put_far(1))], BF16)
        copy = remote(dkv_send.at[col], (dkv_east, dkv_west)[col], lon_send.at[3 + col],
                      lon_recv.at[3 + col], (west, east)[col])
        start(copy)
        returns.append(copy)
    for col in range(2):
        def put_dq(row, value, col=col):
            grad_ref[0, row, col] = value
        from_windows(col, [(get_window(dq_win, col), put_dq)], BF16)

    def finish(half):
        rows = pl.ds(half * HALF, HALF)

        def body(index, carry):
            cols = pl.ds(pl.multiple_of(index * 512, 512), 512)
            mixed_ref[rows, cols] = (
                part[pos, half, :, cols].astype(F32)
                + from_far[pos, half, :, cols].astype(F32)
                + jnp.where(inner, from_near[0, half, :, cols].astype(F32), 0.0)
            ).astype(BF16)
            return carry
        lax.fori_loop(0, D // 512, body, 0)

    @pl.when(edge)
    def _():
        from_near[0] = jnp.zeros_like(from_near[0])
    for half in range(2):
        @pl.when(inner)
        def _():
            wait_near(1, half)
            wait_far(1, half)

        @pl.when(edge)
        def _():
            wait_far(0, half)
        finish(half)

    for col in range(2):
        returns[1 - col].wait_recv()
        came = (dkv_west, dkv_east)[col]

        def put_sum(which, col=col, came=came):
            def write(row, value):
                grad_ref[1 + which, row, col] = (value + came[which, row].astype(F32)).astype(BF16)
            return write
        from_windows(col, [(get_window(dk_own, col), put_sum(0)), (get_window(dv_own, col), put_sum(1))], F32)

    for copy, condition in pending:
        if condition is None:
            copy.wait_send()
        else:
            pl.when(condition)(copy.wait_send)


def per_device(n_lon, qkv, windows, out_weight, cotangent):
    tile_rows = jnp.where(windows[0] < 2 * ROWS, windows[0] // 2, windows[0] - 2 * ROWS) // 2
    odd = (jnp.max(tile_rows) != jnp.min(tile_rows)).astype(BF16)
    mask = jnp.broadcast_to(odd, (TILE, WIDTH))
    vmem = pl.BlockSpec(memory_space=pltpu.VMEM)
    dma = pltpu.SemaphoreType.DMA
    column = (2, ROWS, TILE, WIDTH)
    mixed, grad = pl.pallas_call(
        functools.partial(kernel, n_lon),
        out_shape=(
            jax.ShapeDtypeStruct((OWN, D), BF16),
            jax.ShapeDtypeStruct((3, ROWS, 2, TILE, WIDTH), BF16),
        ),
        in_specs=[vmem] * 4,
        out_specs=(vmem, vmem),
        scratch_shapes=[
            pltpu.VMEM((TILE, WIDTH), BF16),
            pltpu.VMEM(column, BF16),
            pltpu.VMEM(column, BF16),
            pltpu.VMEM((8, 2, HALF, D), BF16),
            pltpu.VMEM((ROWS, 2, TILE, WIDTH), BF16),
            pltpu.VMEM((2, 512, WIDTH), BF16),
            pltpu.VMEM((2, 1024, WIDTH), BF16),
            pltpu.VMEM((2, 1024, WIDTH), BF16),
            pltpu.VMEM((2, 512, WIDTH), BF16),
            pltpu.VMEM((2, 2, 512, HEAD_DIM), F32),
            pltpu.VMEM((2, 512, WIDTH), BF16),
            pltpu.VMEM((ROWS, 2, TILE, WIDTH), BF16),
            pltpu.VMEM((2, 512, WIDTH), BF16),
            pltpu.VMEM((2, 512, WIDTH), F32),
            pltpu.VMEM((2, 512, WIDTH), F32),
            pltpu.VMEM((2, 512, WIDTH), BF16),
            pltpu.VMEM((2, 512, WIDTH), BF16),
            pltpu.VMEM((2,) + column, BF16),
            pltpu.VMEM(column, BF16),
            pltpu.VMEM(column, BF16),
            pltpu.VMEM((4, 2, HALF, D), BF16),
            pltpu.VMEM((4, 2, HALF, D), BF16),
            pltpu.VMEM((4, 2, HALF, D), BF16),
            pltpu.VMEM((3, 2, HALF, D), BF16),
            pltpu.VMEM((2, 2, HALF, D), BF16),
            dma((5,)), dma((5,)), dma((10,)), dma((8,)), dma((8,)), dma((8,)),
            dma((4,)), dma((4,)), dma((6,)), dma((10,)),
        ],
        compiler_params=pltpu.CompilerParams(
            collective_id=0, has_side_effects=True, vmem_limit_bytes=48 * 1024 * 1024
        ),
        cost_estimate=pl.CostEstimate(
            flops=2 * 1270 * 10**6, bytes_accessed=6 * 2**20, transcendentals=2**18
        ),
    )(mask, qkv.reshape(3, ROWS, 2, TILE, WIDTH), out_weight, cotangent)
    return mixed, grad.reshape(3, ROWS * 2 * TILE, WIDTH)


def solution(mesh):
    in_specs = (P(None, "lon", "tp"), P("lon", None), P("tp", None), P(("lon", "tp"), None))
    out_specs = (P(("lon", "tp"), None), P(None, "lon", "tp"))
    return jax.shard_map(
        functools.partial(per_device, mesh.shape["lon"]),
        mesh=mesh, in_specs=in_specs, out_specs=out_specs, check_vma=False,
    )
```

time: 288 us -> 140 us (0.49)
  the two profiles are of different devices: /device:TPU:1 before, /device:TPU:9 now
where the time goes in v1:
time: 140 us
  Pallas kernels  131 us (94%)
  local copies, waits for them, and re-layouts  6.41 us (5%)
  between operations  1.96 us (1%)
    pallas_call x1, Pallas kernels, per_device(): pl.pallas_call(functools.partial(kernel, n_lon), out_shape=(jax.ShapeDtyp...  131 us
    unnamed x8, local copies, waits for them, and re-layouts  5.61 us

profile of v1, /device:TPU:9, one launch (start us, length us, event | category | flops | bytes accessed | tf_op | source)
XLA Modules:
  0.0 140.2 jit_solution(18309555914987192872)
XLA Ops:
  0.6 0.8 slice_reduce_fusion
  1.4 0.7 fusion
  3.4 0.0 copy-start
  3.4 1.4 copy-done
  4.8 0.0 copy-start.1
  4.8 1.2 copy-done.1
  6.0 0.0 copy-start.2
  6.0 1.0 copy-done.2
  7.1 131.2 %shard_map.59 = (bf16[128,2048]{1,0:T(8,128)(2,1)S(1)}, bf16[3,16,2,32,256]{4,3,2,1,0:T(8,128)(2,1)S(1)}) custom-call(bf16[32,256]{1,0:T(8,128)(2,1)S(1)} %broadcast_in_dim.3.mask_ref, bf16[3,16,2,32,256]{4,3,2,1,0:T(8,128)(2,1)S(1)} %bitcast.3, bf16[256,2048]{1,0:T(8,128)(2,1)S(1)} %copy-done.1, bf16[128,2048]{1,0:T(8,128)(2,1)S(1)} %copy-done.2), custom_call_target="tpu_custom_call" | custom-call | flops 2540000000 | bytes 6291456 | tf_op jit(solution)/shard_map/pallas_call | solution.py:456
  138.3 0.8 copy.8
  139.0 1.1 copy.9
  (1 shorter events, 0.0 us)
Async XLA Ops:
  3.4 1.4 %copy-start = (bf16[3,1024,256]{2,1,0:T(8,128)(2,1)S(1)}, bf16[3,1024,256]{2,1,0:T(8,128)(2,1)}, u32[]{:S(2)}) copy-start(bf16[3,1024,256]{2,1,0:T(8,128)(2,1)} %param.4) | copy-start | bytes 4718596
  4.8 1.2 copy-start.1
  6.0 1.0 copy-start.2

commit v2 on v1

--- a/solution.py
+++ b/solution.py
@@ -14,6 +14,8 @@
 WIDTH = 256
 D = 2048
 OWN = 128
+FORWARD_WINDOWS = 2
+BACKWARD_WINDOWS = 2
 HALF = 64
 SCALE = HEAD_DIM ** (-0.5)
 MESH = pl.DeviceIdType.MESH
@@ -31,18 +33,24 @@
 
 def kernel(
     n_lon,
-    mask_ref, qkv_ref, weight_ref, cot_ref,
+    windows_hbm, qkv_hbm, weight_hbm, cot_hbm,
     mixed_ref, grad_ref,
-    west_mask, kv_east, kv_west, gathered, grad_out, q_win, k_win, v_win, do_win,
-    weights, out_win, attended, dq_win, dk_own, dv_own, dk_far, dv_far,
-    dkv_send, dkv_east, dkv_west, part_out, part_in, part, from_near, from_far,
-    lon_send, lon_recv, tp_send, tp_recv, sib_send, sib_recv,
+    windows_ref, qkv_ref, weight_ref, mask_ref, west_mask, relay_west, relay_east, kv_east, kv_west, gathered, grad_out, q_win, k_win, v_win, do_win,
+    weights, out_win, attended, dq_win, dk_own, dv_own,
+    dkv_send, dkv_east, dkv_west, parts, part_in, from_near, from_far,
+    load_sem, mask_send, mask_recv, lon_send, lon_recv, piece_send, piece_recv,
+    relay_send, relay_recv, tp_send, tp_recv, sib_send, sib_recv,
     part_send, part_recv, sum_send, sum_recv,
 ):
     lon, tp = lax.axis_index("lon"), lax.axis_index("tp")
     chip, core = tp // 2, tp % 2
+    depth = lax.rem(lon, 8)
+    first, last = depth == 0, depth == 7
+    column_base = lon - depth
     east = {"lon": lax.rem(lon + 1, n_lon)}
     west = {"lon": lax.rem(lon + n_lon - 1, n_lon)}
+    over_west = lax.rem(column_base + n_lon - 1, n_lon)
+    over_east = lax.rem(column_base + 8, n_lon)
     flip = chip // 2
     pos = chip + flip * (3 - 2 * chip)
     edge, inner = pos == 0, pos == 1
@@ -58,20 +66,48 @@
     far = {"tp": device_at(2, core)}
     sibling = {"tp": 2 * chip + 1 - core}
 
+    loads = [
+        pltpu.make_async_copy(src, dst, load_sem.at[index])
+        for index, (src, dst) in enumerate((
+            (windows_hbm, windows_ref), (cot_hbm, gathered.at[tp]), (weight_hbm, weight_ref), (qkv_hbm, qkv_ref),
+        ))
+    ]
+    for load in loads:
+        load.start()
+
     barrier = pltpu.get_barrier_semaphore()
-    for target in (east, west, sibling):
+
+    def greet(target):
         pl.semaphore_signal(barrier, inc=1, device_id=target, device_id_type=MESH)
 
-    @pl.when(edge)
-    def _():
-        pl.semaphore_signal(barrier, inc=1, device_id=one, device_id_type=MESH)
-        pl.semaphore_wait(barrier, 4)
+    def greet_column(base):
+        def body(index, carry):
+            greet({"lon": base + index})
+            return carry
+        lax.fori_loop(0, 8, body, 0)
+
+    greet(sibling)
+    pl.when(edge)(lambda: greet(one))
 
     @pl.when(inner)
     def _():
-        pl.semaphore_signal(barrier, inc=1, device_id=near, device_id_type=MESH)
-        pl.semaphore_signal(barrier, inc=1, device_id=far, device_id_type=MESH)
-        pl.semaphore_wait(barrier, 5)
+        greet(near)
+        greet(far)
+
+    @pl.when(jnp.logical_not(first))
+    def _():
+        greet(west)
+        greet({"lon": column_base})
+
+    @pl.when(jnp.logical_not(last))
+    def _():
+        greet(east)
+        greet({"lon": column_base + 7})
+
+    pl.when(first)(lambda: greet_column(over_west - 7))
+    pl.when(last)(lambda: greet_column(over_east))
+    at_end = jnp.logical_or(first, last)
+    pl.semaphore_wait(barrier, 2 + jnp.where(inner, 1, 0) + jnp.where(at_end, 10, 4))
 
     def remote(src, dst, send_sem, recv_sem, target):
         return pltpu.make_async_remote_copy(
@@ -88,18 +124,76 @@
             pl.when(condition)(copy.start)
         pending.append((copy, condition))
 
-    mask_copy = remote(mask_ref, west_mask, lon_send.at[0], lon_recv.at[0], east)
-    start(mask_copy)
-    to_west = remote(qkv_ref.at[pl.ds(1, 2), :, 0], kv_east, lon_send.at[1], lon_recv.at[1], west)
-    to_east = remote(qkv_ref.at[pl.ds(1, 2), :, 1], kv_west, lon_send.at[2], lon_recv.at[2], east)
-    start(to_west)
-    start(to_east)
+    def exchange(which, src_west, dst_east, src_east, dst_west, places, rows_from):
+        count = len(places)
+        stride = 8 // count
+
+        def rows(ref, index):
+            return ref.at[:, pl.ds(2 * (rows_from + index), 2)]
+
+        def whole(ref):
+            return ref.at[:, pl.ds(2 * rows_from, 2 * count)]
+
+        direct_west = remote(whole(src_west), whole(dst_east), lon_send.at[2 * which],
+                             lon_recv.at[2 * which], west)
+        direct_east = remote(whole(src_east), whole(dst_west), lon_send.at[2 * which + 1],
+                             lon_recv.at[2 * which + 1], east)
+        mine = depth // stride
+        relays = lax.rem(depth, stride) == places[0]
+        sides = ((0, src_west, dst_east, relay_west, first, 0), (1, src_east, dst_west, relay_east, last, 7))
+
+        def over(src, dst, side, condition, index):
+            start(remote(src, rows(dst, index), relay_send.at[which, side],
+                         piece_recv.at[which, index], {"lon": (over_west, over_east)[side]}), condition)
+
+        def launch():
+            for side, src, dst, relay, end, own_place in sides:
+                for index, place in sorted(enumerate(places), key=lambda item: abs(item[1] - own_place) % 7):
+                    if place == own_place:
+                        over(rows(src, index), dst, side, end, index)
+                    else:
+                        start(remote(rows(src, index), relay.at[which], piece_send.at[which, index],
+                                     relay_recv.at[which, side], {"lon": column_base + place}), end)
+            start(direct_west, jnp.logical_not(first))
+            start(direct_east, jnp.logical_not(last))
+
+        def forward_pieces():
+            for side, src, dst, relay, end, own_place in sides:
+                condition = jnp.logical_and(relays, jnp.logical_not(end))
+
+                @pl.when(condition)
+                def _():
+                    remote(relay.at[which], relay.at[which], relay_send.at[which, side],
+                           relay_recv.at[which, side], sibling).wait_recv()
+                over(relay.at[which], dst, side, condition, mine)
+
+        def wait_from(side):
+            copy, dst, at_column_end = ((direct_east, dst_west, first), (direct_west, dst_east, last))[side]
+            pl.when(jnp.logical_not(at_column_end))(copy.wait_recv)
+
+            @pl.when(at_column_end)
+            def _():
+                for index in range(count):
+                    remote(rows(dst, index), rows(dst, index), relay_send.at[which, 0],
+                           piece_recv.at[which, index], sibling).wait_recv()
+
+        return launch, forward_pieces, wait_from
+
+    send_kv, relay_kv, wait_kv = exchange(
+        0, qkv_hbm.at[pl.ds(1, 2), :, 0], kv_east, qkv_hbm.at[pl.ds(1, 2), :, 1], kv_west, list(range(8)), 0
+    )
+    returns = [
+        exchange(1 + stage, dkv_send.at[0], dkv_east, dkv_send.at[1], dkv_west,
+                 list(range(stage, 8, 2)), 4 * stage)
+        for stage in range(2)
+    ]
+    send_kv()
 
     def block(place, which, half):
         return gathered.at[device_at(place, which), half]
 
     def own_half(half):
-        return cot_ref.at[pl.ds(half * HALF, HALF)]
+        return cot_hbm.at[half]
 
     def slot(place, half):
         return 2 * place + half
@@ -170,23 +264,15 @@
             dst = gathered.at[device_at(place_of(order), 1 - core), half]
             remote(dst, dst, sib_send.at[0], sib_recv.at[2 * order + half], sibling).wait_recv()
 
-    def project_back(src_rows, device):
-        def body(index, carry):
-            rows = src_rows(index)
-            value = dot(rows, weight_ref[...], NT).astype(BF16)
-            grad_out[2 * device + index] = value.reshape(2, TILE, WIDTH)
-            return carry
-        lax.fori_loop(0, 2, body, 0)
+    def project_back(order):
+        source = chip_at(place_of(order))
+        rows = gathered[pl.ds(2 * source, 2)].reshape(2 * OWN, D)
+        value = dot(rows, weight_ref[...], NT).astype(BF16)
+        grad_out[pl.ds(4 * source, 4)] = value.reshape(4, 2, TILE, WIDTH)
 
     def project_order(order):
-        if order == 0:
-            project_back(lambda i: cot_ref[pl.ds(i * HALF, HALF), :], tp)
-        else:
-            device = device_at(place_of(order), core)
-            project_back(lambda i: gathered[device, i], device)
         wait_hand_over(order)
-        other = device_at(place_of(order), 1 - core)
-        project_back(lambda i: gathered[other, i], other)
+        project_back(order)
 
     def mask_of(col):
         return (west_mask, mask_ref)[col]
@@ -238,53 +324,71 @@
             (lambda row: kv[1, row], put_key(v_win, col, 1)),
         ])
 
+    UNITS = [(col, head) for col in range(2) for head in range(2)]
+
+    def unit(ref, col, head, place):
+        return ref[col, place, head * HEAD_DIM:(head + 1) * HEAD_DIM]
+
     def forward():
-        def body(window, carry):
-            qs = pl.ds(pl.multiple_of(window * 64, 64), 64)
-            ks = pl.ds(pl.multiple_of(window * 128, 128), 128)
-            for col in range(2):
-                for head in range(2):
-                    lanes = slice(head * HEAD_DIM, (head + 1) * HEAD_DIM)
-                    scores = dot(q_win[col, qs, lanes], k_win[col, ks, lanes], NT) * SCALE
-                    raised = jnp.exp(scores - jnp.max(scores, axis=-1, keepdims=True))
-                    probs = raised / jnp.sum(raised, axis=-1, keepdims=True)
-                    weights[col, head, qs, :] = probs
-                    out_win[col, qs, lanes] = dot(
-                        probs.astype(BF16), v_win[col, ks, lanes], NN
-                    ).astype(BF16)
-            return carry
-        lax.fori_loop(0, WINDOWS, body, 0)
-
-    def backward():
-        def body(window, carry):
-            qs = pl.ds(pl.multiple_of(window * 64, 64), 64)
-            ks = pl.ds(pl.multiple_of(window * 128, 128), 128)
-            for col in range(2):
-                for head in range(2):
-                    lanes = slice(head * HEAD_DIM, (head + 1) * HEAD_DIM)
-                    probs = weights[col, head, qs, :]
-                    d_out = do_win[col, qs, lanes]
-                    grad_w = dot(d_out, v_win[col, ks, lanes], NT)
-                    row_dot = jnp.sum(probs * grad_w, axis=-1, keepdims=True)
-                    grad_s = (probs * (grad_w - row_dot) * SCALE).astype(BF16)
-                    dq_win[col, qs, lanes] = dot(grad_s, k_win[col, ks, lanes], NN).astype(BF16)
-                    dk = dot(grad_s, q_win[col, qs, lanes], TN)
-                    dv = dot(probs.astype(BF16), d_out, TN)
-                    dk_own[col, qs, lanes] = dk[:64]
-                    dv_own[col, qs, lanes] = dv[:64]
-                    dk_far[col, qs, lanes] = dk[64:].astype(BF16)
-                    dv_far[col, qs, lanes] = dv[64:].astype(BF16)
-            return carry
-        lax.fori_loop(0, WINDOWS, body, 0)
-
-    def project(rows_of, dst):
-        rows = attended[pl.ds(2 * rows_of, 2)].reshape(OWN, WIDTH)
+        def body(step, carry):
+            spots = []
+            for sub in range(FORWARD_WINDOWS):
+                window = step * FORWARD_WINDOWS + sub
+                qs = pl.ds(pl.multiple_of(window * 64, 64), 64)
+                ks = pl.ds(pl.multiple_of(window * 128, 128), 128)
+                spots += [(col, head, qs, ks) for col, head in UNITS]
+            values = [unit(v_win, col, head, ks) for col, head, qs, ks in spots]
+            scores = [
+                dot(unit(q_win, col, head, qs), unit(k_win, col, head, ks), NT) * SCALE
+                for col, head, qs, ks in spots
+            ]
+            raised = [jnp.exp(x - jnp.max(x, axis=-1, keepdims=True)) for x in scores]
+            probs = [x / jnp.sum(x, axis=-1, keepdims=True) for x in raised]
+            outs = [dot(x.astype(BF16), v, NN).astype(BF16) for x, v in zip(probs, values)]
+            for (col, head, qs, ks), x, out in zip(spots, probs, outs):
+                weights[col, head, qs, :] = x
+                out_win[col, qs, head * HEAD_DIM:(head + 1) * HEAD_DIM] = out
+            return carry
+        lax.fori_loop(0, WINDOWS // FORWARD_WINDOWS, body, 0)
+
+    def backward(stage):
+        def body(step, carry):
+            spots = []
+            for sub in range(BACKWARD_WINDOWS):
+                slot_at = stage * 4 + step * BACKWARD_WINDOWS + sub
+                window = lax.rem(slot_at + 3 * flip, WINDOWS)
+                qs = pl.ds(pl.multiple_of(window * 64, 64), 64)
+                ks = pl.ds(pl.multiple_of(window * 128, 128), 128)
+                spots += [(col, head, qs, ks, slot_at) for col, head in UNITS]
+            queries = [unit(q_win, col, head, qs) for col, head, qs, ks, _ in spots]
+            keys = [unit(k_win, col, head, ks) for col, head, qs, ks, _ in spots]
+            d_outs = [unit(do_win, col, head, qs) for col, head, qs, ks, _ in spots]
+            probs = [weights[col, head, qs, :] for col, head, qs, ks, _ in spots]
+            grad_w = [
+                dot(d, unit(v_win, col, head, ks), NT) for d, (col, head, qs, ks, _) in zip(d_outs, spots)
+            ]
+            dvs = [dot(x.astype(BF16), d, TN) for x, d in zip(probs, d_outs)]
+            row_dots = [jnp.sum(x * g, axis=-1, keepdims=True) for x, g in zip(probs, grad_w)]
+            grad_s = [(x * (g - r) * SCALE).astype(BF16) for x, g, r in zip(probs, grad_w, row_dots)]
+            dqs = [dot(g, k, NN).astype(BF16) for g, k in zip(grad_s, keys)]
+            dks = [dot(g, q, TN) for g, q in zip(grad_s, queries)]
+            for (col, head, qs, ks, slot_at), dq, dk, dv in zip(spots, dqs, dks, dvs):
+                lanes = slice(head * HEAD_DIM, (head + 1) * HEAD_DIM)
+                dq_win[col, qs, lanes] = dq
+                dk_own[col, qs, lanes] = dk[:64]
+                dv_own[col, qs, lanes] = dv[:64]
+                dkv_send[col, 0, pl.ds(2 * slot_at, 2), :, lanes] = dk[64:].astype(BF16).reshape(2, TILE, HEAD_DIM)
+                dkv_send[col, 1, pl.ds(2 * slot_at, 2), :, lanes] = dv[64:].astype(BF16).reshape(2, TILE, HEAD_DIM)
+            return carry
+        lax.fori_loop(0, 4 // BACKWARD_WINDOWS, body, 0)
+
+    def project(place):
+        rows = attended[pl.ds(4 * chip_at(place), 4)].reshape(2 * OWN, WIDTH)
 
         def body(index, carry):
             cols = pl.ds(pl.multiple_of(index * 512, 512), 512)
             value = dot(rows, weight_ref[:, cols], NN).astype(BF16)
-            dst[0, :, cols] = value[:HALF]
-            dst[1, :, cols] = value[HALF:]
+            parts[place, :, :, :, cols] = value.reshape(2, 2, HALF, 512)
             return carry
         lax.fori_loop(0, D // 512, body, 0)
 
@@ -295,19 +399,21 @@
             return carry
         lax.fori_loop(0, D // 512, body, 0)
 
+    def part(place, half):
+        return parts.at[place, core, half]
+
     def part_copy(place):
-        return remote(part_out.at[place], part_in.at[place], part_send.at[place],
+        return remote(parts.at[place, 1 - core], part_in.at[place], part_send.at[place],
                       part_recv.at[place], sibling)
 
     def partials(place):
-        project(device_at(place, 1 - core), part_out.at[place])
+        project(place)
         start(part_copy(place))
-        project(device_at(place, core), part.at[place])
 
     def join_cores(place):
         part_copy(place).wait_recv()
         for half in range(2):
-            add(part.at[place, half], part_in.at[place, half])
+            add(part(place, half), part_in.at[place, half])
 
     def near_sem(place, half):
         return sum_recv.at[2 * (place - 1) + half]
@@ -317,7 +423,7 @@
 
     def send_edge(place):
         for half in range(2):
-            start(remote(part.at[place, half], from_near.at[place - 1, half],
+            start(remote(part(place, half), from_near.at[place - 1, half],
                          sum_send.at[2 * (place - 1) + half], near_sem(place, half), one), edge)
 
     def wait_near(place, half):
@@ -332,28 +438,38 @@
         @pl.when(inner)
         def _():
             wait_near(place, half)
-            add(part.at[place, half], from_near.at[place - 1, half])
-        start(remote(part.at[place, half], from_far.at[3 - place, half],
+            add(part(place, half), from_near.at[place - 1, half])
+        start(remote(part(place, half), from_far.at[3 - place, half],
                      sum_send.at[2 * (place - 2) + half], far_sem(3 - place, half), far), inner)
 
     def pass_near(half):
         @pl.when(inner)
         def _():
             wait_far(0, half)
-            add(part.at[0, half], from_far.at[0, half])
-        start(remote(part.at[0, half], from_far.at[0, half],
+            add(part(0, half), from_far.at[0, half])
+        start(remote(part(0, half), from_far.at[0, half],
                      sum_send.at[4 + half], far_sem(0, half), near), inner)
 
+    loads[0].wait()
+    tiles = windows_ref[...]
+    tile_rows = jnp.where(tiles < 2 * ROWS, tiles // 4, (tiles - 2 * ROWS) // 2)
+    odd = jnp.max(tile_rows, axis=0, keepdims=True) != jnp.min(tile_rows, axis=0, keepdims=True)
+    mask_ref[...] = jnp.broadcast_to(odd[:, :1].astype(F32), (TILE, WIDTH)).astype(BF16)
+    mask_copy = remote(mask_ref, west_mask, mask_send.at[0], mask_recv.at[0], east)
+    start(mask_copy)
+    for load in loads[1:]:
+        load.wait()
+    own_into_windows(1)
     project_order(0)
-    own_into_windows(1)
+    relay_kv()
     mask_copy.wait_recv()
     own_into_windows(0)
     gather_step(1, 0)
     gather_step(1, 1)
     project_order(1)
-    to_west.wait_recv()
+    wait_kv(1)
     far_into_windows(1)
-    to_east.wait_recv()
+    wait_kv(0)
     far_into_windows(0)
     forward()
     gather_step(2, 0)
@@ -363,40 +479,39 @@
         from_windows(col, [(get_window(out_win, col), put_attended)], BF16)
     partials(3)
     partials(2)
+    partials(0)
     join_cores(3)
     send_edge(3)
-    gather_step(2, 1)
-    partials(0)
     partials(1)
     join_cores(2)
     send_edge(2)
+    gather_step(2, 1)
     join_cores(1)
     send_edge(1)
     join_cores(0)
+
+    def grad_out_into_windows():
+        for col in range(2):
+            into_windows(col, [(lambda row, col=col: grad_out[row, col], put_query(do_win, col))])
+
     project_order(2)
+    grad_out_into_windows()
+    backward(0)
+    returns[0][0]()
+    pass_far(3, 0)
     gather_step(3, 0)
-    pass_far(3, 0)
+    pass_far(3, 1)
     gather_step(3, 1)
-    pass_far(3, 1)
+    returns[0][1]()
     project_order(3)
-    for col in range(2):
-        into_windows(col, [(lambda row, col=col: grad_out[row, col], put_query(do_win, col))])
+    grad_out_into_windows()
+    backward(1)
+    returns[1][0]()
     pass_near(0)
     pass_far(2, 0)
     pass_near(1)
     pass_far(2, 1)
-    backward()
-    returns = []
-    for col in range(2):
-        def put_far(which, col=col):
-            def write(row, value):
-                dkv_send[col, which, row] = value
-            return write
-        from_windows(col, [(get_window(dk_far, col), put_far(0)), (get_window(dv_far, col), put_far(1))], BF16)
-        copy = remote(dkv_send.at[col], (dkv_east, dkv_west)[col], lon_send.at[3 + col],
-                      lon_recv.at[3 + col], (west, east)[col])
-        start(copy)
-        returns.append(copy)
+    returns[1][1]()
     for col in range(2):
         def put_dq(row, value, col=col):
             grad_ref[0, row, col] = value
@@ -408,7 +523,7 @@
         def body(index, carry):
             cols = pl.ds(pl.multiple_of(index * 512, 512), 512)
             mixed_ref[rows, cols] = (
-                part[pos, half, :, cols].astype(F32)
+                parts[pos, core, half, :, cols].astype(F32)
                 + from_far[pos, half, :, cols].astype(F32)
                 + jnp.where(inner, from_near[0, half, :, cols].astype(F32), 0.0)
             ).astype(BF16)
@@ -430,14 +545,20 @@
         finish(half)
 
     for col in range(2):
-        returns[1 - col].wait_recv()
+        for stage in range(2):
+            returns[stage][2](col)
         came = (dkv_west, dkv_east)[col]
 
-        def put_sum(which, col=col, came=came):
+        def put_sum(which, col=col):
             def write(row, value):
-                grad_ref[1 + which, row, col] = (value + came[which, row].astype(F32)).astype(BF16)
+                grad_ref[1 + which, row, col] = value.astype(BF16)
             return write
-        from_windows(col, [(get_window(dk_own, col), put_sum(0)), (get_window(dv_own, col), put_sum(1))], F32)
+
+        def get_sum(which, ref, col=col, came=came):
+            own = get_window(ref, col)
+            return lambda row: own(row) + came[which, lax.rem(row + 10 * flip, ROWS)].astype(F32)
+
+        from_windows(col, [(get_sum(0, dk_own), put_sum(0)), (get_sum(1, dv_own), put_sum(1))], F32)
 
     for copy, condition in pending:
         if condition is None:
@@ -447,10 +568,8 @@
 
 
 def per_device(n_lon, qkv, windows, out_weight, cotangent):
-    tile_rows = jnp.where(windows[0] < 2 * ROWS, windows[0] // 2, windows[0] - 2 * ROWS) // 2
-    odd = (jnp.max(tile_rows) != jnp.min(tile_rows)).astype(BF16)
-    mask = jnp.broadcast_to(odd, (TILE, WIDTH))
     vmem = pl.BlockSpec(memory_space=pltpu.VMEM)
+    anywhere = pl.BlockSpec(memory_space=pl.ANY)
     dma = pltpu.SemaphoreType.DMA
     column = (2, ROWS, TILE, WIDTH)
     mixed, grad = pl.pallas_call(
@@ -459,10 +578,16 @@
             jax.ShapeDtypeStruct((OWN, D), BF16),
             jax.ShapeDtypeStruct((3, ROWS, 2, TILE, WIDTH), BF16),
         ),
-        in_specs=[vmem] * 4,
+        in_specs=[anywhere] * 4,
         out_specs=(vmem, vmem),
         scratch_shapes=[
+            pltpu.VMEM((4, WINDOWS), jnp.int32),
+            pltpu.VMEM((3, ROWS, 2, TILE, WIDTH), BF16),
+            pltpu.VMEM((WIDTH, D), BF16),
             pltpu.VMEM((TILE, WIDTH), BF16),
+            pltpu.VMEM((TILE, WIDTH), BF16),
+            pltpu.VMEM((3, 2, 2, TILE, WIDTH), BF16),
+            pltpu.VMEM((3, 2, 2, TILE, WIDTH), BF16),
             pltpu.VMEM(column, BF16),
             pltpu.VMEM(column, BF16),
             pltpu.VMEM((8, 2, HALF, D), BF16),
@@ -477,26 +602,24 @@
             pltpu.VMEM((2, 512, WIDTH), BF16),
             pltpu.VMEM((2, 512, WIDTH), F32),
             pltpu.VMEM((2, 512, WIDTH), F32),
-            pltpu.VMEM((2, 512, WIDTH), BF16),
-            pltpu.VMEM((2, 512, WIDTH), BF16),
             pltpu.VMEM((2,) + column, BF16),
             pltpu.VMEM(column, BF16),
             pltpu.VMEM(column, BF16),
-            pltpu.VMEM((4, 2, HALF, D), BF16),
-            pltpu.VMEM((4, 2, HALF, D), BF16),
+            pltpu.VMEM((4, 2, 2, HALF, D), BF16),
             pltpu.VMEM((4, 2, HALF, D), BF16),
             pltpu.VMEM((3, 2, HALF, D), BF16),
             pltpu.VMEM((2, 2, HALF, D), BF16),
-            dma((5,)), dma((5,)), dma((10,)), dma((8,)), dma((8,)), dma((8,)),
+            dma((4,)), dma((1,)), dma((1,)), dma((6,)), dma((6,)), dma((3, 8)), dma((3, 8)),
+            dma((3, 2)), dma((3, 2)), dma((10,)), dma((8,)), dma((8,)), dma((8,)),
             dma((4,)), dma((4,)), dma((6,)), dma((10,)),
         ],
         compiler_params=pltpu.CompilerParams(
-            collective_id=0, has_side_effects=True, vmem_limit_bytes=48 * 1024 * 1024
+            collective_id=0, has_side_effects=True, vmem_limit_bytes=56 * 1024 * 1024
         ),
         cost_estimate=pl.CostEstimate(
             flops=2 * 1270 * 10**6, bytes_accessed=6 * 2**20, transcendentals=2**18
         ),
-    )(mask, qkv.reshape(3, ROWS, 2, TILE, WIDTH), out_weight, cotangent)
+    )(windows.T, qkv.reshape(3, ROWS, 2, TILE, WIDTH), out_weight, cotangent.reshape(2, HALF, D))
     return mixed, grad.reshape(3, ROWS * 2 * TILE, WIDTH)
 
 

time: 140 us -> 107 us (0.76)
  the two profiles are of different devices: /device:TPU:9 before, /device:TPU:1 now
where the time goes in v2:
time: 107 us; the launch traced here: 106 us
  Pallas kernels  101 us (94%)
  local copies, waits for them, and re-layouts  4.53 us (4%)
    pallas_call x1, Pallas kernels, per_device(): pl.pallas_call(functools.partial(kernel, n_lon), out_shape=(jax.ShapeDtyp...  101 us
    unnamed x2, local copies, waits for them, and re-layouts  4.53 us

profile of v2, /device:TPU:1, one launch (start us, length us, event | category | flops | bytes accessed | tf_op | source)
XLA Modules:
  0.0 106.4 jit_solution(4892476475126341243)
XLA Ops:
  0.6 101.2 %shard_map.59 = (bf16[128,2048]{1,0:T(8,128)(2,1)}, bf16[3,16,2,32,256]{4,3,2,1,0:T(8,128)(2,1)}) custom-call(s32[4,8]{1,0:T(4,128)} %bitcast.7, bf16[3,16,2,32,256]{4,3,2,1,0:T(8,128)(2,1)} %bitcast.5, bf16[256,2048]{1,0:T(8,128)(2,1)} %weight_hbm.1, bf16[2,64,2048]{2,1,0:T(8,128)(2,1)} %bitcast.6), custom_call_target="tpu_custom_call" | custom-call | flops 2540000000 | bytes 6291456 | tf_op jit(solution)/shard_map/pallas_call | solution.py:575
  101.8 1.9 %copy.8 = bf16[128,2048]{1,0:T(8,128)(2,1)} copy(bf16[128,2048]{1,0:T(8,128)(2,1)} %get-tuple-element.8) | data formatting | bytes 1048576
  103.7 2.7 %copy.9 = bf16[3,1024,256]{2,1,0:T(8,128)(2,1)} copy(bf16[3,1024,256]{2,1,0:T(8,128)(2,1)} %bitcast.4) | data formatting | bytes 3145728

commit v3 on v2

--- a/solution.py
+++ b/solution.py
@@ -14,7 +14,7 @@
 WIDTH = 256
 D = 2048
 OWN = 128
-FORWARD_WINDOWS = 2
+ORDER = (4, 3, 5, 2, 6, 1, 7, 0)
 BACKWARD_WINDOWS = 2
 HALF = 64
 SCALE = HEAD_DIM ** (-0.5)
@@ -54,6 +54,7 @@
     flip = chip // 2
     pos = chip + flip * (3 - 2 * chip)
     edge, inner = pos == 0, pos == 1
+    edge_chip, inner_chip = edge, inner
 
     def chip_at(place):
         return place + flip * (3 - 2 * place)
@@ -124,22 +125,22 @@
             pl.when(condition)(copy.start)
         pending.append((copy, condition))
 
-    def exchange(which, src_west, dst_east, src_east, dst_west, places, rows_from):
-        count = len(places)
-        stride = 8 // count
+    def exchange(which, src_west, dst_east, src_east, dst_west, row_of, runs):
+        count = 8
 
         def rows(ref, index):
-            return ref.at[:, pl.ds(2 * (rows_from + index), 2)]
-
-        def whole(ref):
-            return ref.at[:, pl.ds(2 * rows_from, 2 * count)]
-
-        direct_west = remote(whole(src_west), whole(dst_east), lon_send.at[2 * which],
-                             lon_recv.at[2 * which], west)
-        direct_east = remote(whole(src_east), whole(dst_west), lon_send.at[2 * which + 1],
-                             lon_recv.at[2 * which + 1], east)
-        mine = depth // stride
-        relays = lax.rem(depth, stride) == places[0]
+            return ref.at[:, pl.ds(row_of(index), 1)]
+
+        def direct(src, dst, side, target):
+            return [
+                remote(src.at[:, pl.ds(begin, length)], dst.at[:, pl.ds(begin, length)],
+                       lon_send.at[which, side, run], lon_recv.at[which, side, run], target)
+                for run, (begin, length) in enumerate(runs)
+            ]
+
+        direct_west = direct(src_west, dst_east, 0, west)
+        direct_east = direct(src_east, dst_west, 1, east)
+
         sides = ((0, src_west, dst_east, relay_west, first, 0), (1, src_east, dst_west, relay_east, last, 7))
 
         def over(src, dst, side, condition, index):
@@ -148,28 +149,35 @@
 
         def launch():
             for side, src, dst, relay, end, own_place in sides:
-                for index, place in sorted(enumerate(places), key=lambda item: abs(item[1] - own_place) % 7):
-                    if place == own_place:
-                        over(rows(src, index), dst, side, end, index)
+                for step in ORDER:
+                    place = abs(own_place - step)
+                    if step == 0:
+                        over(rows(src, place), dst, side, end, place)
                     else:
-                        start(remote(rows(src, index), relay.at[which], piece_send.at[which, index],
+                        start(remote(rows(src, place), relay.at[which], piece_send.at[which, place],
                                      relay_recv.at[which, side], {"lon": column_base + place}), end)
-            start(direct_west, jnp.logical_not(first))
-            start(direct_east, jnp.logical_not(last))
+            for copy in direct_west:
+                start(copy, jnp.logical_not(first))
+            for copy in direct_east:
+                start(copy, jnp.logical_not(last))
 
         def forward_pieces():
             for side, src, dst, relay, end, own_place in sides:
-                condition = jnp.logical_and(relays, jnp.logical_not(end))
+                condition = jnp.logical_not(end)
 
                 @pl.when(condition)
                 def _():
                     remote(relay.at[which], relay.at[which], relay_send.at[which, side],
                            relay_recv.at[which, side], sibling).wait_recv()
-                over(relay.at[which], dst, side, condition, mine)
+                over(relay.at[which], dst, side, condition, depth)
 
         def wait_from(side):
-            copy, dst, at_column_end = ((direct_east, dst_west, first), (direct_west, dst_east, last))[side]
-            pl.when(jnp.logical_not(at_column_end))(copy.wait_recv)
+            copies, dst, at_column_end = ((direct_east, dst_west, first), (direct_west, dst_east, last))[side]
+
+            @pl.when(jnp.logical_not(at_column_end))
+            def _():
+                for copy in copies:
+                    copy.wait_recv()
 
             @pl.when(at_column_end)
             def _():
@@ -179,15 +187,26 @@
 
         return launch, forward_pieces, wait_from
 
-    send_kv, relay_kv, wait_kv = exchange(
-        0, qkv_hbm.at[pl.ds(1, 2), :, 0], kv_east, qkv_hbm.at[pl.ds(1, 2), :, 1], kv_west, list(range(8)), 0
-    )
+    def first_row(index):
+        return jnp.where(index < 6, 10 - 10 * flip + index, 14 * flip + index - 6)
+
+    def second_row(index):
+        return 2 + 4 * flip + index
+
+    kv_halves = [
+        exchange(half, qkv_hbm.at[pl.ds(1, 2), :, 0], kv_east, qkv_hbm.at[pl.ds(1, 2), :, 1], kv_west, row_of, runs)
+        for half, (row_of, runs) in enumerate((
+            (first_row, [(10 - 10 * flip, 6), (14 * flip, 2)]),
+            (second_row, [(2 + 4 * flip, 8)]),
+        ))
+    ]
     returns = [
-        exchange(1 + stage, dkv_send.at[0], dkv_east, dkv_send.at[1], dkv_west,
-                 list(range(stage, 8, 2)), 4 * stage)
+        exchange(2 + stage, dkv_send.at[0], dkv_east, dkv_send.at[1], dkv_west,
+                 lambda index, stage=stage: 8 * stage + index, [(8 * stage, 8)])
         for stage in range(2)
     ]
-    send_kv()
+    kv_halves[0][0]()
+    kv_halves[1][0]()
 
     def block(place, which, half):
         return gathered.at[device_at(place, which), half]
@@ -216,7 +235,11 @@
         src = block(place, core, half)
         return remote(src, src, sib_send.at[2 * order + half], sib_recv.at[2 * order + half], sibling)
 
-    def gather_step(order, half):
+    def gather_step(order, half, where=None):
+        def both(condition):
+            return condition if where is None else jnp.logical_and(condition, where)
+
+        edge, inner = both(edge_chip), both(inner_chip)
         if order == 1:
             @pl.when(edge)
             def _():
@@ -277,23 +300,25 @@
     def mask_of(col):
         return (west_mask, mask_ref)[col]
 
-    def into_windows(col, pairs):
-        def body(row, carry):
+    def into_windows(col, pairs, begin=0, count=ROWS):
+        def body(index, carry):
+            row = lax.rem(begin + index, ROWS)
             later = lax.rem(row + 1, ROWS)
             take = mask_of(col)[...] > 0
             for read, write in pairs:
                 write(row, jnp.where(take, read(later), read(row)))
             return carry
-        lax.fori_loop(0, ROWS, body, 0)
-
-    def from_windows(col, pairs, dtype):
-        def body(row, carry):
+        lax.fori_loop(0, count, body, 0)
+
+    def from_windows(col, pairs, dtype, begin=0, count=ROWS):
+        def body(index, carry):
+            row = lax.rem(begin + index, ROWS)
             before = lax.rem(row + ROWS - 1, ROWS)
             take = mask_of(col)[...].astype(dtype) > 0
             for read, write in pairs:
                 write(row, jnp.where(take, read(before), read(row)))
             return carry
-        lax.fori_loop(0, ROWS, body, 0)
+        lax.fori_loop(0, count, body, 0)
 
     def put_query(ref, col):
         def write(row, value):
@@ -317,39 +342,42 @@
             (lambda row: qkv_ref[2, row, col], put_key(v_win, col, 0)),
         ])
 
-    def far_into_windows(col):
+    def far_into_windows(col, begin, count):
         kv = (kv_west, kv_east)[col]
         into_windows(col, [
             (lambda row: kv[0, row], put_key(k_win, col, 1)),
             (lambda row: kv[1, row], put_key(v_win, col, 1)),
-        ])
+        ], 2 * begin, 2 * count)
 
     UNITS = [(col, head) for col in range(2) for head in range(2)]
 
     def unit(ref, col, head, place):
         return ref[col, place, head * HEAD_DIM:(head + 1) * HEAD_DIM]
 
-    def forward():
-        def body(step, carry):
-            spots = []
-            for sub in range(FORWARD_WINDOWS):
-                window = step * FORWARD_WINDOWS + sub
-                qs = pl.ds(pl.multiple_of(window * 64, 64), 64)
-                ks = pl.ds(pl.multiple_of(window * 128, 128), 128)
-                spots += [(col, head, qs, ks) for col, head in UNITS]
-            values = [unit(v_win, col, head, ks) for col, head, qs, ks in spots]
-            scores = [
-                dot(unit(q_win, col, head, qs), unit(k_win, col, head, ks), NT) * SCALE
-                for col, head, qs, ks in spots
-            ]
-            raised = [jnp.exp(x - jnp.max(x, axis=-1, keepdims=True)) for x in scores]
-            probs = [x / jnp.sum(x, axis=-1, keepdims=True) for x in raised]
-            outs = [dot(x.astype(BF16), v, NN).astype(BF16) for x, v in zip(probs, values)]
-            for (col, head, qs, ks), x, out in zip(spots, probs, outs):
-                weights[col, head, qs, :] = x
-                out_win[col, qs, head * HEAD_DIM:(head + 1) * HEAD_DIM] = out
-            return carry
-        lax.fori_loop(0, WINDOWS // FORWARD_WINDOWS, body, 0)
+    def forward(begin, count):
+        spots = []
+        for sub in range(count):
+            window = lax.rem(begin + sub, WINDOWS)
+            qs = pl.ds(pl.multiple_of(window * 64, 64), 64)
+            ks = pl.ds(pl.multiple_of(window * 128, 128), 128)
+            spots += [(col, head, qs, ks) for col, head in UNITS]
+        values = [unit(v_win, col, head, ks) for col, head, qs, ks in spots]
+        scores = [
+            dot(unit(q_win, col, head, qs), unit(k_win, col, head, ks), NT) * SCALE
+            for col, head, qs, ks in spots
+        ]
+        raised = [jnp.exp(x - jnp.max(x, axis=-1, keepdims=True)) for x in scores]
+        probs = [x / jnp.sum(x, axis=-1, keepdims=True) for x in raised]
+        outs = [dot(x.astype(BF16), v, NN).astype(BF16) for x, v in zip(probs, values)]
+        for (col, head, qs, ks), x, out in zip(spots, probs, outs):
+            weights[col, head, qs, :] = x
+            out_win[col, qs, head * HEAD_DIM:(head + 1) * HEAD_DIM] = out
+
+    def attend(begin, count):
+        for col in range(2):
+            def put_attended(row, value, col=col):
+                attended[row, col] = value
+            from_windows(col, [(get_window(out_win, col), put_attended)], BF16, begin, count)
 
     def backward(stage):
         def body(step, carry):
@@ -460,35 +488,44 @@
     for load in loads[1:]:
         load.wait()
     own_into_windows(1)
-    project_order(0)
-    relay_kv()
+    kv_halves[0][1]()
     mask_copy.wait_recv()
     own_into_windows(0)
+    kv_halves[1][1]()
+    inside = jnp.logical_not(at_end)
     gather_step(1, 0)
-    gather_step(1, 1)
+    gather_step(1, 1, at_end)
+    near_window = 5 + 2 * flip
+    for col in (1, 0):
+        kv_halves[0][2](col)
+        far_into_windows(col, near_window, 3)
+    forward(near_window, 3)
+    attend(4 * chip_at(3), 4)
+    partials(3)
+    gather_step(1, 1, inside)
+    join_cores(3)
+    send_edge(3)
+    project_order(0)
     project_order(1)
-    wait_kv(1)
-    far_into_windows(1)
-    wait_kv(0)
-    far_into_windows(0)
-    forward()
-    gather_step(2, 0)
-    for col in range(2):
-        def put_attended(row, value, col=col):
-            attended[row, col] = value
-        from_windows(col, [(get_window(out_win, col), put_attended)], BF16)
-    partials(3)
+    gather_step(2, 0, at_end)
+    for col in (1, 0):
+        kv_halves[1][2](col)
+        far_into_windows(col, near_window + 3, 5)
+    forward(near_window + 3, 3)
+    forward(near_window + 6, 2)
+    attend(4 * chip_at(3) + 4, 12)
+    gather_step(2, 0, inside)
     partials(2)
     partials(0)
-    join_cores(3)
-    send_edge(3)
     partials(1)
     join_cores(2)
     send_edge(2)
-    gather_step(2, 1)
+    pass_far(3, 0)
     join_cores(1)
     send_edge(1)
     join_cores(0)
+    gather_step(2, 1)
+    pass_far(3, 1)
 
     def grad_out_into_windows():
         for col in range(2):
@@ -498,17 +535,15 @@
     grad_out_into_windows()
     backward(0)
     returns[0][0]()
-    pass_far(3, 0)
     gather_step(3, 0)
-    pass_far(3, 1)
+    pass_near(0)
     gather_step(3, 1)
-    returns[0][1]()
+    pass_far(2, 0)
     project_order(3)
     grad_out_into_windows()
     backward(1)
     returns[1][0]()
-    pass_near(0)
-    pass_far(2, 0)
+    returns[0][1]()
     pass_near(1)
     pass_far(2, 1)
     returns[1][1]()
@@ -569,7 +604,6 @@
 
 def per_device(n_lon, qkv, windows, out_weight, cotangent):
     vmem = pl.BlockSpec(memory_space=pltpu.VMEM)
-    anywhere = pl.BlockSpec(memory_space=pl.ANY)
     dma = pltpu.SemaphoreType.DMA
     column = (2, ROWS, TILE, WIDTH)
     mixed, grad = pl.pallas_call(
@@ -578,7 +612,7 @@
             jax.ShapeDtypeStruct((OWN, D), BF16),
             jax.ShapeDtypeStruct((3, ROWS, 2, TILE, WIDTH), BF16),
         ),
-        in_specs=[anywhere] * 4,
+        in_specs=[pl.BlockSpec(memory_space=pltpu.HBM)] * 4,
         out_specs=(vmem, vmem),
         scratch_shapes=[
             pltpu.VMEM((4, WINDOWS), jnp.int32),
@@ -586,8 +620,8 @@
             pltpu.VMEM((WIDTH, D), BF16),
             pltpu.VMEM((TILE, WIDTH), BF16),
             pltpu.VMEM((TILE, WIDTH), BF16),
-            pltpu.VMEM((3, 2, 2, TILE, WIDTH), BF16),
-            pltpu.VMEM((3, 2, 2, TILE, WIDTH), BF16),
+            pltpu.VMEM((4, 2, 1, TILE, WIDTH), BF16),
+            pltpu.VMEM((4, 2, 1, TILE, WIDTH), BF16),
             pltpu.VMEM(column, BF16),
             pltpu.VMEM(column, BF16),
             pltpu.VMEM((8, 2, HALF, D), BF16),
@@ -609,12 +643,12 @@
             pltpu.VMEM((4, 2, HALF, D), BF16),
             pltpu.VMEM((3, 2, HALF, D), BF16),
             pltpu.VMEM((2, 2, HALF, D), BF16),
-            dma((4,)), dma((1,)), dma((1,)), dma((6,)), dma((6,)), dma((3, 8)), dma((3, 8)),
-            dma((3, 2)), dma((3, 2)), dma((10,)), dma((8,)), dma((8,)), dma((8,)),
+            dma((4,)), dma((1,)), dma((1,)), dma((4, 2, 2)), dma((4, 2, 2)), dma((4, 8)), dma((4, 8)),
+            dma((4, 2)), dma((4, 2)), dma((10,)), dma((8,)), dma((8,)), dma((8,)),
             dma((4,)), dma((4,)), dma((6,)), dma((10,)),
         ],
         compiler_params=pltpu.CompilerParams(
-            collective_id=0, has_side_effects=True, vmem_limit_bytes=56 * 1024 * 1024
+            collective_id=0, has_side_effects=True, vmem_limit_bytes=53 * 1024 * 1024
         ),
         cost_estimate=pl.CostEstimate(
             flops=2 * 1270 * 10**6, bytes_accessed=6 * 2**20, transcendentals=2**18

time: 107 us -> 97.7 us (0.913)
  Pallas kernels: 101 us -> 92.8 us
    pallas_call x1, Pallas kernels: 101 us -> 92.8 us  [per_device(): pl.pallas_call(functools.partial(kernel, n_lon), out_shape=(jax.ShapeDtyp...]
    unnamed x2 -> x4, local copies, waits for them, and re-layouts: 4.53 us -> 4.12 us
where the time goes in v3:
time: 97.7 us; the launch traced here: 97.5 us
  Pallas kernels  92.8 us (95%)
  local copies, waits for them, and re-layouts  4.12 us (4%)
    pallas_call x1, Pallas kernels, per_device(): pl.pallas_call(functools.partial(kernel, n_lon), out_shape=(jax.ShapeDtyp...  92.8 us
    unnamed x4, local copies, waits for them, and re-layouts  4.12 us

profile of v3, /device:TPU:1, one launch (start us, length us, event | category | flops | bytes accessed | tf_op | source)
XLA Modules:
  0.0 97.5 jit_solution(14847086042387465099)
XLA Ops:
  0.6 0.0 copy-start
  0.6 0.7 copy-done
  1.3 92.8 %shard_map.59 = (bf16[128,2048]{1,0:T(8,128)(2,1)S(1)}, bf16[3,16,2,32,256]{4,3,2,1,0:T(8,128)(2,1)}) custom-call(s32[4,8]{1,0:T(4,128)S(1)} %bitcast.4, bf16[3,16,2,32,256]{4,3,2,1,0:T(8,128)(2,1)} %bitcast.6, bf16[256,2048]{1,0:T(8,128)(2,1)} %weight_hbm.1, bf16[2,64,2048]{2,1,0:T(8,128)(2,1)} %bitcast.7), custom_call_target="tpu_custom_call" | custom-call | flops 2540000000 | bytes 6291456 | tf_op jit(solution)/shard_map/pallas_call | solution.py:609
  94.1 0.8 copy.8
  94.9 2.7 %copy.9 = bf16[3,1024,256]{2,1,0:T(8,128)(2,1)} copy(bf16[3,1024,256]{2,1,0:T(8,128)(2,1)} %bitcast.5) | data formatting | bytes 3145728
Async XLA Ops:
  0.6 0.7 copy-start

commit v4 on v3

--- a/solution.py
+++ b/solution.py
@@ -15,7 +15,6 @@
 D = 2048
 OWN = 128
 ORDER = (4, 3, 5, 2, 6, 1, 7, 0)
-BACKWARD_WINDOWS = 2
 HALF = 64
 SCALE = HEAD_DIM ** (-0.5)
 MESH = pl.DeviceIdType.MESH
@@ -125,11 +124,9 @@
             pl.when(condition)(copy.start)
         pending.append((copy, condition))
 
-    def exchange(which, src_west, dst_east, src_east, dst_west, row_of, runs):
-        count = 8
-
-        def rows(ref, index):
-            return ref.at[:, pl.ds(row_of(index), 1)]
+    def exchange(which, src_west, dst_east, src_east, dst_west, shares, runs):
+        def rows(ref, share, place):
+            return ref.at[:, pl.ds(share[2](place), share[1])]
 
         def direct(src, dst, side, target):
             return [
@@ -143,18 +140,24 @@
 
         sides = ((0, src_west, dst_east, relay_west, first, 0), (1, src_east, dst_west, relay_east, last, 7))
 
-        def over(src, dst, side, condition, index):
-            start(remote(src, rows(dst, index), relay_send.at[which, side],
-                         piece_recv.at[which, index], {"lon": (over_west, over_east)[side]}), condition)
+        def over(src, dst, side, condition, share, place):
+            start(remote(src, rows(dst, share, place), relay_send.at[which, side],
+                         piece_recv.at[which, place], {"lon": (over_west, over_east)[side]}), condition)
+
+        def passing(relay, share):
+            return relay.at[which, :, pl.ds(0, share[1])]
 
         def launch():
             for side, src, dst, relay, end, own_place in sides:
                 for step in ORDER:
                     place = abs(own_place - step)
+                    share = next((item for item in shares if place in item[0]), None)
+                    if share is None:
+                        continue
                     if step == 0:
-                        over(rows(src, place), dst, side, end, place)
+                        over(rows(src, share, place), dst, side, end, share, place)
                     else:
-                        start(remote(rows(src, place), relay.at[which], piece_send.at[which, place],
+                        start(remote(rows(src, share, place), passing(relay, share), piece_send.at[which, place],
                                      relay_recv.at[which, side], {"lon": column_base + place}), end)
             for copy in direct_west:
                 start(copy, jnp.logical_not(first))
@@ -163,13 +166,16 @@
 
         def forward_pieces():
             for side, src, dst, relay, end, own_place in sides:
-                condition = jnp.logical_not(end)
-
-                @pl.when(condition)
-                def _():
-                    remote(relay.at[which], relay.at[which], relay_send.at[which, side],
-                           relay_recv.at[which, side], sibling).wait_recv()
-                over(relay.at[which], dst, side, condition, depth)
+                for share in shares:
+                    among = functools.reduce(jnp.logical_or, [depth == place for place in share[0]])
+                    condition = jnp.logical_and(among, jnp.logical_not(end))
+                    piece = passing(relay, share)
+
+                    @pl.when(condition)
+                    def _():
+                        remote(piece, piece, relay_send.at[which, side],
+                               relay_recv.at[which, side], sibling).wait_recv()
+                    over(piece, dst, side, condition, share, depth)
 
         def wait_from(side):
             copies, dst, at_column_end = ((direct_east, dst_west, first), (direct_west, dst_east, last))[side]
@@ -181,9 +187,10 @@
 
             @pl.when(at_column_end)
             def _():
-                for index in range(count):
-                    remote(rows(dst, index), rows(dst, index), relay_send.at[which, 0],
-                           piece_recv.at[which, index], sibling).wait_recv()
+                for share in shares:
+                    for place in share[0]:
+                        ref = rows(dst, share, place)
+                        remote(ref, ref, relay_send.at[which, 0], piece_recv.at[which, place], sibling).wait_recv()
 
         return launch, forward_pieces, wait_from
 
@@ -194,19 +201,22 @@
         return 2 + 4 * flip + index
 
     kv_halves = [
-        exchange(half, qkv_hbm.at[pl.ds(1, 2), :, 0], kv_east, qkv_hbm.at[pl.ds(1, 2), :, 1], kv_west, row_of, runs)
+        exchange(half, qkv_hbm.at[pl.ds(1, 2), :, 0], kv_east, qkv_hbm.at[pl.ds(1, 2), :, 1], kv_west,
+                 [(range(8), 1, row_of)], runs)
         for half, (row_of, runs) in enumerate((
             (first_row, [(10 - 10 * flip, 6), (14 * flip, 2)]),
             (second_row, [(2 + 4 * flip, 8)]),
         ))
     ]
+    return_shares = (
+        [((0, 7), 2, lambda place: 2 * (place // 7)), (range(1, 7), 1, lambda place: 3 + place)],
+        [((0, 1, 2, 5, 6, 7), 1, lambda place: 10 + place - 2 * (place // 5))],
+    )
     returns = [
-        exchange(2 + stage, dkv_send.at[0], dkv_east, dkv_send.at[1], dkv_west,
-                 lambda index, stage=stage: 8 * stage + index, [(8 * stage, 8)])
-        for stage in range(2)
+        exchange(2 + stage, dkv_send.at[0], dkv_east, dkv_send.at[1], dkv_west, return_shares[stage], [run])
+        for stage, run in enumerate(((0, 10), (10, 6)))
     ]
     kv_halves[0][0]()
-    kv_halves[1][0]()
 
     def block(place, which, half):
         return gathered.at[device_at(place, which), half]
@@ -217,7 +227,7 @@
     def slot(place, half):
         return 2 * place + half
 
-    for half in range(2):
+    def send_own(half):
         start(remote(own_half(half), gathered.at[tp, half], tp_send.at[half],
                      tp_recv.at[slot(0, half)], one), edge)
         start(remote(own_half(half), gathered.at[tp, half], tp_send.at[half],
@@ -226,6 +236,8 @@
                      tp_recv.at[slot(2, half)], far), inner)
         start(remote(own_half(half), gathered.at[tp, half], sib_send.at[half],
                      sib_recv.at[half], sibling))
+
+    send_own(0)
 
     def wait_tp(place, half):
         remote(block(place, core, half), block(place, core, half), tp_send.at[0],
@@ -379,36 +391,33 @@
                 attended[row, col] = value
             from_windows(col, [(get_window(out_win, col), put_attended)], BF16, begin, count)
 
-    def backward(stage):
-        def body(step, carry):
-            spots = []
-            for sub in range(BACKWARD_WINDOWS):
-                slot_at = stage * 4 + step * BACKWARD_WINDOWS + sub
-                window = lax.rem(slot_at + 3 * flip, WINDOWS)
-                qs = pl.ds(pl.multiple_of(window * 64, 64), 64)
-                ks = pl.ds(pl.multiple_of(window * 128, 128), 128)
-                spots += [(col, head, qs, ks, slot_at) for col, head in UNITS]
-            queries = [unit(q_win, col, head, qs) for col, head, qs, ks, _ in spots]
-            keys = [unit(k_win, col, head, ks) for col, head, qs, ks, _ in spots]
-            d_outs = [unit(do_win, col, head, qs) for col, head, qs, ks, _ in spots]
-            probs = [weights[col, head, qs, :] for col, head, qs, ks, _ in spots]
-            grad_w = [
-                dot(d, unit(v_win, col, head, ks), NT) for d, (col, head, qs, ks, _) in zip(d_outs, spots)
-            ]
-            dvs = [dot(x.astype(BF16), d, TN) for x, d in zip(probs, d_outs)]
-            row_dots = [jnp.sum(x * g, axis=-1, keepdims=True) for x, g in zip(probs, grad_w)]
-            grad_s = [(x * (g - r) * SCALE).astype(BF16) for x, g, r in zip(probs, grad_w, row_dots)]
-            dqs = [dot(g, k, NN).astype(BF16) for g, k in zip(grad_s, keys)]
-            dks = [dot(g, q, TN) for g, q in zip(grad_s, queries)]
-            for (col, head, qs, ks, slot_at), dq, dk, dv in zip(spots, dqs, dks, dvs):
-                lanes = slice(head * HEAD_DIM, (head + 1) * HEAD_DIM)
-                dq_win[col, qs, lanes] = dq
-                dk_own[col, qs, lanes] = dk[:64]
-                dv_own[col, qs, lanes] = dv[:64]
-                dkv_send[col, 0, pl.ds(2 * slot_at, 2), :, lanes] = dk[64:].astype(BF16).reshape(2, TILE, HEAD_DIM)
-                dkv_send[col, 1, pl.ds(2 * slot_at, 2), :, lanes] = dv[64:].astype(BF16).reshape(2, TILE, HEAD_DIM)
-            return carry
-        lax.fori_loop(0, 4 // BACKWARD_WINDOWS, body, 0)
+    def backward(begin, count):
+        spots = []
+        for sub in range(count):
+            slot_at = begin + sub
+            window = lax.rem(slot_at + 2 * flip, WINDOWS)
+            qs = pl.ds(pl.multiple_of(window * 64, 64), 64)
+            ks = pl.ds(pl.multiple_of(window * 128, 128), 128)
+            spots += [(col, head, qs, ks, slot_at) for col, head in UNITS]
+        queries = [unit(q_win, col, head, qs) for col, head, qs, ks, _ in spots]
+        keys = [unit(k_win, col, head, ks) for col, head, qs, ks, _ in spots]
+        d_outs = [unit(do_win, col, head, qs) for col, head, qs, ks, _ in spots]
+        probs = [weights[col, head, qs, :] for col, head, qs, ks, _ in spots]
+        grad_w = [
+            dot(d, unit(v_win, col, head, ks), NT) for d, (col, head, qs, ks, _) in zip(d_outs, spots)
+        ]
+        dvs = [dot(x.astype(BF16), d, TN) for x, d in zip(probs, d_outs)]
+        row_dots = [jnp.sum(x * g, axis=-1, keepdims=True) for x, g in zip(probs, grad_w)]
+        grad_s = [(x * (g - r) * SCALE).astype(BF16) for x, g, r in zip(probs, grad_w, row_dots)]
+        dqs = [dot(g, k, NN).astype(BF16) for g, k in zip(grad_s, keys)]
+        dks = [dot(g, q, TN) for g, q in zip(grad_s, queries)]
+        for (col, head, qs, ks, slot_at), dq, dk, dv in zip(spots, dqs, dks, dvs):
+            lanes = slice(head * HEAD_DIM, (head + 1) * HEAD_DIM)
+            dq_win[col, qs, lanes] = dq
+            dk_own[col, qs, lanes] = dk[:64]
+            dv_own[col, qs, lanes] = dv[:64]
+            dkv_send[col, 0, pl.ds(2 * slot_at, 2), :, lanes] = dk[64:].astype(BF16).reshape(2, TILE, HEAD_DIM)
+            dkv_send[col, 1, pl.ds(2 * slot_at, 2), :, lanes] = dv[64:].astype(BF16).reshape(2, TILE, HEAD_DIM)
 
     def project(place):
         rows = attended[pl.ds(4 * chip_at(place), 4)].reshape(2 * OWN, WIDTH)
@@ -489,11 +498,13 @@
         load.wait()
     own_into_windows(1)
     kv_halves[0][1]()
+    kv_halves[1][0]()
+    send_own(1)
     mask_copy.wait_recv()
     own_into_windows(0)
-    kv_halves[1][1]()
     inside = jnp.logical_not(at_end)
     gather_step(1, 0)
+    kv_halves[1][1]()
     gather_step(1, 1, at_end)
     near_window = 5 + 2 * flip
     for col in (1, 0):
@@ -533,7 +544,8 @@
 
     project_order(2)
     grad_out_into_windows()
-    backward(0)
+    backward(0, 3)
+    backward(3, 2)
     returns[0][0]()
     gather_step(3, 0)
     pass_near(0)
@@ -541,7 +553,8 @@
     pass_far(2, 0)
     project_order(3)
     grad_out_into_windows()
-    backward(1)
+    backward(5, 3)
+    early = len(pending)
     returns[1][0]()
     returns[0][1]()
     pass_near(1)
@@ -552,6 +565,34 @@
             grad_ref[0, row, col] = value
         from_windows(col, [(get_window(dq_win, col), put_dq)], BF16)
 
+    def drain(copies):
+        for copy, condition in copies:
+            if condition is None:
+                copy.wait_send()
+            else:
+                pl.when(condition)(copy.wait_send)
+
+    def add_returns(stage):
+        begin, count = ((4 * flip + 1, 9), (4 * flip + 10, 7))[stage]
+        for col in range(2):
+            returns[stage][2](col)
+            came = (dkv_west, dkv_east)[col]
+
+            def put_sum(which, col=col):
+                def write(row, value):
+                    grad_ref[1 + which, row, col] = value.astype(BF16)
+                return write
+
+            def get_sum(which, ref, col=col, came=came):
+                own = get_window(ref, col)
+                return lambda row: own(row) + came[which, lax.rem(row + 12 * flip, ROWS)].astype(F32)
+
+            from_windows(col, [(get_sum(0, dk_own), put_sum(0)), (get_sum(1, dv_own), put_sum(1))], F32,
+                         begin, count)
+
+    drain(pending[:early])
+    add_returns(0)
+
     def finish(half):
         rows = pl.ds(half * HALF, HALF)
 
@@ -579,27 +620,8 @@
             wait_far(0, half)
         finish(half)
 
-    for col in range(2):
-        for stage in range(2):
-            returns[stage][2](col)
-        came = (dkv_west, dkv_east)[col]
-
-        def put_sum(which, col=col):
-            def write(row, value):
-                grad_ref[1 + which, row, col] = value.astype(BF16)
-            return write
-
-        def get_sum(which, ref, col=col, came=came):
-            own = get_window(ref, col)
-            return lambda row: own(row) + came[which, lax.rem(row + 10 * flip, ROWS)].astype(F32)
-
-        from_windows(col, [(get_sum(0, dk_own), put_sum(0)), (get_sum(1, dv_own), put_sum(1))], F32)
-
-    for copy, condition in pending:
-        if condition is None:
-            copy.wait_send()
-        else:
-            pl.when(condition)(copy.wait_send)
+    add_returns(1)
+    drain(pending[early:])
 
 
 def per_device(n_lon, qkv, windows, out_weight, cotangent):
@@ -620,8 +642,8 @@
             pltpu.VMEM((WIDTH, D), BF16),
             pltpu.VMEM((TILE, WIDTH), BF16),
             pltpu.VMEM((TILE, WIDTH), BF16),
-            pltpu.VMEM((4, 2, 1, TILE, WIDTH), BF16),
-            pltpu.VMEM((4, 2, 1, TILE, WIDTH), BF16),
+            pltpu.VMEM((4, 2, 2, TILE, WIDTH), BF16),
+            pltpu.VMEM((4, 2, 2, TILE, WIDTH), BF16),
             pltpu.VMEM(column, BF16),
             pltpu.VMEM(column, BF16),
             pltpu.VMEM((8, 2, HALF, D), BF16),

time: 97.7 us -> 96.4 us (0.987)
  Pallas kernels: 92.8 us -> 91.4 us
    pallas_call x1, Pallas kernels: 92.8 us -> 91.4 us  [per_device(): pl.pallas_call(functools.partial(kernel, n_lon), out_shape=(jax.ShapeDtyp...]
where the time goes in v4:
time: 96.4 us; the launch traced here: 96.2 us
  Pallas kernels  91.4 us (95%)
  local copies, waits for them, and re-layouts  4.12 us (4%)
    pallas_call x1, Pallas kernels, per_device(): pl.pallas_call(functools.partial(kernel, n_lon), out_shape=(jax.ShapeDtyp...  91.4 us
    unnamed x4, local copies, waits for them, and re-layouts  4.12 us

profile of v4, /device:TPU:1, one launch (start us, length us, event | category | flops | bytes accessed | tf_op | source)
XLA Modules:
  0.0 96.2 jit_solution(14498301062739575046)
XLA Ops:
  0.6 0.0 copy-start
  0.6 0.7 copy-done
  1.3 91.4 %shard_map.59 = (bf16[128,2048]{1,0:T(8,128)(2,1)S(1)}, bf16[3,16,2,32,256]{4,3,2,1,0:T(8,128)(2,1)}) custom-call(s32[4,8]{1,0:T(4,128)S(1)} %bitcast.4, bf16[3,16,2,32,256]{4,3,2,1,0:T(8,128)(2,1)} %bitcast.6, bf16[256,2048]{1,0:T(8,128)(2,1)} %weight_hbm.1, bf16[2,64,2048]{2,1,0:T(8,128)(2,1)} %bitcast.7), custom_call_target="tpu_custom_call" | custom-call | flops 2540000000 | bytes 6291456 | tf_op jit(solution)/shard_map/pallas_call | solution.py:631
  92.8 0.8 copy.8
  93.6 2.7 %copy.9 = bf16[3,1024,256]{2,1,0:T(8,128)(2,1)} copy(bf16[3,1024,256]{2,1,0:T(8,128)(2,1)} %bitcast.5) | data formatting | bytes 3145728
Async XLA Ops:
  0.6 0.7 copy-start

commit v5 on v4

--- a/solution.py
+++ b/solution.py
@@ -536,7 +536,6 @@
     send_edge(1)
     join_cores(0)
     gather_step(2, 1)
-    pass_far(3, 1)
 
     def grad_out_into_windows():
         for col in range(2):
@@ -547,6 +546,7 @@
     backward(0, 3)
     backward(3, 2)
     returns[0][0]()
+    pass_far(3, 1)
     gather_step(3, 0)
     pass_near(0)
     gather_step(3, 1)

time: 96.4 us -> 96.4 us (level)
  no operation moved by 1% of the time
where the time goes in v5:
time: 96.4 us; the launch traced here: 96.2 us
  Pallas kernels  91.4 us (95%)
  local copies, waits for them, and re-layouts  4.12 us (4%)
    pallas_call x1, Pallas kernels, per_device(): pl.pallas_call(functools.partial(kernel, n_lon), out_shape=(jax.ShapeDtyp...  91.4 us
    unnamed x4, local copies, waits for them, and re-layouts  4.12 us

profile of v5, /device:TPU:1, one launch (start us, length us, event | category | flops | bytes accessed | tf_op | source)
XLA Modules:
  0.0 96.2 jit_solution(784486604271345228)
XLA Ops:
  0.6 0.0 copy-start
  0.6 0.7 copy-done
  1.3 91.4 %shard_map.59 = (bf16[128,2048]{1,0:T(8,128)(2,1)S(1)}, bf16[3,16,2,32,256]{4,3,2,1,0:T(8,128)(2,1)}) custom-call(s32[4,8]{1,0:T(4,128)S(1)} %bitcast.4, bf16[3,16,2,32,256]{4,3,2,1,0:T(8,128)(2,1)} %bitcast.6, bf16[256,2048]{1,0:T(8,128)(2,1)} %weight_hbm.1, bf16[2,64,2048]{2,1,0:T(8,128)(2,1)} %bitcast.7), custom_call_target="tpu_custom_call" | custom-call | flops 2540000000 | bytes 6291456 | tf_op jit(solution)/shard_map/pallas_call | solution.py:631
  92.8 0.8 copy.8
  93.6 2.7 %copy.9 = bf16[3,1024,256]{2,1,0:T(8,128)(2,1)} copy(bf16[3,1024,256]{2,1,0:T(8,128)(2,1)} %bitcast.5) | data formatting | bytes 3145728
Async XLA Ops:
  0.6 0.7 copy-start
